TPU v7x, 32 devices: a whole 2x2x4 slice. The times are simulated.
32 devices in a mesh: parts: 2 (over x), docs: 16 (over z, y, core).
Axes of the slice: x: 2, y: 2, z: 4, core: 2. Of those that a mesh axis runs over, the one named last changes fastest.
Arguments:
- doc_grads: bfloat16 [4096, 8192], P('parts', 'docs'), parts along dimension 0, may hold values from -6 to 6
- query_grads: bfloat16 [16384, 8192], P(('parts', 'docs')), parts along dimension 0, may hold values from -6 to 6
- left_inv: bfloat16 [2, 32, 32], replicated, may hold values from -17 to 17, as said below
- right_inv: bfloat16 [2, 128, 128], replicated, may hold values from -17 to 17, as said below
- cand_owner: int32 [8192, 1], P(('parts', 'docs')), parts along dimension 0, may hold values from 0 to 15; in each aligned block of 256 rows (0 to 255, 256 to 511, ...) at most 32 rows name the same one
- cand_row: int32 [8192], P(('parts', 'docs')), parts along dimension 0, may hold values from 0 to 127
Outputs:
- scores: float32 [16384, 256], P(('parts', 'docs')), parts along dimension 0
There are 2 independent parts, one for each index of `parts`. A program takes and returns all parts, laid end to end along the dimension named above; an argument that names none is the same for every part. Nothing has to cross between parts.
Inputs may be any that keep to these rules, and one draw needn't show every extreme that they name: `cand_owner`: within the 256 entries of one query batch no owner is named more than 32 times, a bound that some block reaches. `left_inv`: symmetric positive definite. `right_inv`: symmetric positive definite.
All inputs are finite; a program needn't handle non-finite values.
Results may differ from a plain program's by a relative error of at most 0.004.
Values may be sent and summed in bfloat16 or wider, within the bound.
No kernel may reach another device: no remote copies, remote signals or barrier semaphores. Data moves between devices by JAX's collectives and lax.ppermute only.
A program may use at most 128 MiB of HBM per device.

v0:
```python
import jax
import jax.numpy as jnp
from jax import lax
from jax.sharding import PartitionSpec as P


def precondition(queries, left_inv, right_inv):
    total = queries.shape[0]
    k_out = left_inv.shape[1]
    k_in = right_inv.shape[1]
    block_size = k_out * k_in
    pieces = []
    for layer_index in range(left_inv.shape[0]):
        block = queries[:, layer_index * block_size : (layer_index + 1) * block_size].reshape(
            total, k_out, k_in
        )
        middle = jnp.einsum(
            "qij,jk->qik", block, right_inv[layer_index], preferred_element_type=jnp.float32
        ).astype(jnp.bfloat16)
        result = jnp.einsum(
            "ai,qik->qak", left_inv[layer_index], middle, preferred_element_type=jnp.float32
        ).astype(jnp.bfloat16)
        pieces.append(result.reshape(total, block_size))
    return jnp.concatenate(pieces, axis=1)


def on_device(doc_grads, query_grads, left_inv, right_inv, cand_owner, cand_row):
    devices = lax.axis_size("docs")
    doc_count = doc_grads.shape[0] // devices
    requests = cand_row.shape[0]
    owners = cand_owner[:, 0]
    every_owner, every_row = (
        lax.all_gather(owners, "docs", axis=0, tiled=True),
        lax.all_gather(cand_row, "docs", axis=0, tiled=True),
    )
    doc_ids = (every_owner * doc_count + every_row).reshape(devices, requests)
    pieces = jnp.take(doc_grads, doc_ids, axis=0)
    chosen = lax.all_to_all(pieces, "docs", split_axis=0, concat_axis=2, tiled=True)[0]
    prepared = precondition(query_grads, left_inv, right_inv)
    scores = jnp.einsum("qf,cf->qc", prepared, chosen, preferred_element_type=jnp.float32)
    return scores * prepared.shape[1] ** (-0.5)


def solution(mesh):
    placed = (
        P("parts", "docs"),
        P(("parts", "docs"), None),
        P(),
        P(),
        P(("parts", "docs"), None),
        P(("parts", "docs")),
    )
    return jax.shard_map(
        on_device, mesh=mesh, in_specs=placed, out_specs=P(("parts", "docs"), None), check_vma=False
    )
```

profile of v0, /device:TPU:15, one launch (start us, length us, event | category | flops | bytes accessed | tf_op | source)
XLA Modules:
  0.0 173.4 jit_solution(16309065107494575158)
XLA Ops:
  0.0 0.0 copy-start
  0.0 15.9 %all-gather = s32[4096,1]{0,1:T(1,128)S(1)} all-gather(s32[256,1]{0,1:T(1,128)} %param.10), channel_id=2, replica_groups=mesh['parts'=2,'docs'=16] {'docs'}, dimensions={0}, use_global_device_ids=true | all-gather | bytes 17408 | tf_op jit(solution)/shard_map/all_gather | solution.py:33
  16.0 21.6 %all-gather.1 = s32[16,1,256]{2,1,0:T(1,128)S(1)} all-gather(s32[1,1,256]{2,1,0:T(1,128)} %bitcast.56), channel_id=1, replica_groups=mesh['parts'=2,'docs'=16] {'docs'}, dimensions={0}, use_global_device_ids=true | all-gather | bytes 17408 | tf_op jit(solution)/shard_map/all_gather | solution.py:34
  37.6 0.0 copy-done
  37.6 17.3 %gather_fusion = bf16[4096,512]{1,0:T(8,128)(2,1)} fusion(bf16[2048,512]{1,0:T(8,128)(2,1)S(1)} %copy-done, s32[4096]{0:T(1024)S(1)} %broadcast_clamp_fusion), kind=kCustom, calls=%fused_computation | custom fusion | bytes 8404992 | tf_op jit(solution)/shard_map/jit(_take)/gather | solution.py:37
  55.0 6.4 %copy.8 = bf16[16,256,512]{1,2,0:T(8,128)(2,1)} copy(bf16[16,256,512]{2,1,0:T(8,128)(2,1)} %bitcast.48) | data formatting | bytes 8388608 | tf_op jit(solution)/shard_map/jit(_take)/gather | solution.py:37
  61.4 4.6 %broadcast_select_fusion = bf16[16,256,512]{1,2,0:T(8,128)(2,1)} fusion(bf16[16,256,512]{1,2,0:T(8,128)(2,1)} %copy.8, pred[16,256]{1,0:T(8,128)(4,1)S(1)} %compare_and_fusion), kind=kLoop, calls=%fused_computation.13 | loop fusion | flops 2097152 | bytes 8392704 | tf_op jit(solution)/shard_map/jit(_take)/select_n | solution.py:37
  66.0 7.2 %all-to-all-start = ((bf16[16,256,512]{1,2,0:T(8,128)(2,1)}), bf16[16,256,512]{1,2,0:T(8,128)(2,1)}, u32[]{:S(2)}, u32[]{:S(2)}) async-start(bf16[16,256,512]{1,2,0:T(8,128)(2,1)} %broadcast_select_fusion), calls=%async_computation | async-start | bytes 8388608 | tf_op jit(solution)/shard_map/all_to_all | solution.py:38
  73.1 3.8 %slice_bitcast_fusion.1 = (bf16[64,8,32,128]{3,1,2,0:T(8,128)(2,1)S(1)}, bf16[64,8,32,128]{3,1,2,0:T(8,128)(2,1)S(1)}) fusion(bf16[512,8192]{1,0:T(8,128)(2,1)} %param.7), kind=kLoop, calls=%fused_computation.12 | loop fusion | bytes 16777216
  76.9 3.2 %copy.9 = bf16[64,8,32,128]{3,2,1,0:T(8,128)(2,1)} copy(bf16[64,8,32,128]{3,1,2,0:T(8,128)(2,1)S(1)} %get-tuple-element.5) | data formatting | bytes 8388608
  80.2 0.0 copy-start.1
  80.2 0.0 copy-start.2
  80.2 3.2 %copy.11 = bf16[64,8,32,128]{3,2,1,0:T(8,128)(2,1)} copy(bf16[64,8,32,128]{3,1,2,0:T(8,128)(2,1)S(1)} %get-tuple-element.6) | data formatting | bytes 8388608
  83.4 0.0 copy-done.1
  83.4 0.0 copy-done.2
  83.4 6.6 %fusion.12 = bf16[512,128,32]{1,2,0:T(8,128)(2,1)} fusion(bf16[512,32,128]{2,1,0:T(8,128)(2,1)} %bitcast.49, bf16[2,128,128]{2,1,0:T(8,128)(2,1)S(1)} %copy-done.1, bf16[2,32,32]{2,1,0:T(8,128)(2,1)S(1)} %copy-done.2), kind=kOutput, calls=%fused_computation.16 | convolution fusion | flops 675282944 | bytes 8429568 | tf_op jit(solution)/shard_map/ai,qik->qak/dot_general | solution.py:20
  90.0 6.6 %fusion.15 = bf16[512,128,32]{1,2,0:T(8,128)(2,1)} fusion(bf16[512,32,128]{2,1,0:T(8,128)(2,1)} %bitcast.50, bf16[2,128,128]{2,1,0:T(8,128)(2,1)S(1)} %copy-done.1, bf16[2,32,32]{2,1,0:T(8,128)(2,1)S(1)} %copy-done.2), kind=kOutput, calls=%fused_computation.17 | convolution fusion | flops 675282944 | bytes 8429568 | tf_op jit(solution)/shard_map/ai,qik->qak/dot_general | solution.py:20
  96.6 13.1 %copy_bitcast_fusion = (bf16[512,4096]{1,0:T(8,128)(2,1)}, bf16[512,4096]{1,0:T(8,128)(2,1)}) fusion(bf16[64,8,32,128]{3,2,1,0:T(8,128)(2,1)} %bitcast.52, bf16[64,8,32,128]{3,2,1,0:T(8,128)(2,1)} %bitcast.51), kind=kLoop, calls=%fused_computation.5 | loop fusion | bytes 16777216 | tf_op jit(solution)/shard_map/reshape | solution.py:23
  109.7 55.9 %all-to-all-done = bf16[16,256,512]{1,2,0:T(8,128)(2,1)} async-done(((bf16[16,256,512]{1,2,0:T(8,128)(2,1)}), bf16[16,256,512]{1,2,0:T(8,128)(2,1)}, u32[]{:S(2)}, u32[]{:S(2)}) %all-to-all-start) | async-done | bytes 4194336 | tf_op jit(solution)/shard_map/all_to_all | solution.py:38
  165.6 7.8 %fusion.18 = f32[512,256]{1,0:T(8,128)} fusion(bf16[256,8192]{0,1:T(8,128)(2,1)} %bitcast.16, bf16[512,4096]{1,0:T(8,128)(2,1)} %get-tuple-element.7, bf16[512,4096]{1,0:T(8,128)(2,1)} %get-tuple-element.8), kind=kOutput, calls=%fused_computation.18 | convolution fusion | flops 2164391936 | bytes 13107200 | tf_op jit(solution)/shard_map/qf,cf->qc/dot_general | solution.py:40
  (8 shorter events, 0.1 us)
Async XLA Ops:
  0.0 37.6 %copy-start = (bf16[2048,512]{1,0:T(8,128)(2,1)S(1)}, bf16[2048,512]{1,0:T(8,128)(2,1)}, u32[]{:S(2)}) copy-start(bf16[2048,512]{1,0:T(8,128)(2,1)} %param.6) | copy-start | bytes 6291460
  66.0 99.7 %all-to-all-start = ((bf16[16,256,512]{1,2,0:T(8,128)(2,1)}), bf16[16,256,512]{1,2,0:T(8,128)(2,1)}, u32[]{:S(2)}, u32[]{:S(2)}) async-start(bf16[16,256,512]{1,2,0:T(8,128)(2,1)} %broadcast_select_fusion), calls=%async_computation | async-start | bytes 8388608 | tf_op jit(solution)/shard_map/all_to_all | solution.py:38
  80.2 3.2 %copy-start.1 = (bf16[2,128,128]{2,1,0:T(8,128)(2,1)S(1)}, bf16[2,128,128]{2,1,0:T(8,128)(2,1)}, u32[]{:S(2)}) copy-start(bf16[2,128,128]{2,1,0:T(8,128)(2,1)} %param.9) | copy-start | bytes 196612
  80.2 3.2 %copy-start.2 = (bf16[2,32,32]{2,1,0:T(8,128)(2,1)S(1)}, bf16[2,32,32]{2,1,0:T(8,128)(2,1)}, u32[]{:S(2)}) copy-start(bf16[2,32,32]{2,1,0:T(8,128)(2,1)} %param.8) | copy-start | bytes 12292
where the time goes:
time: 174 us; the launch traced here: 173 us
  waiting for transfers between devices  55.9 us (32%)
  local copies, waits for them, and re-layouts  47.2 us (27%)
  blocking collectives  37.5 us (22%)
  matrix products  21 us (12%)
  starting transfers between devices  7.19 us (4%)
  other arithmetic  4.59 us (3%)
    all_to_all x1, waiting for transfers between devices, on_device(): lax.all_to_all(pieces, 'docs', split_axis=0, concat_axis=2, tiled=True)[0]  55.9 us
    gather x2, local copies, waits for them, and re-layouts, on_device(): pieces = jnp.take(doc_grads, doc_ids, axis=0)  23.8 us
    all_gather x1, blocking collectives, on_device(): lax.all_gather(cand_row, 'docs', axis=0, tiled=True)  21.6 us
    all_gather x1, blocking collectives, on_device(): lax.all_gather(owners, 'docs', axis=0, tiled=True)  15.9 us
    dot_general x2, matrix products, precondition(): jnp.einsum('ai,qik->qak', left_inv[layer_index], middle, preferred_elemen...  13.2 us
    reshape x1, local copies, waits for them, and re-layouts, precondition(): pieces.append(result.reshape(total, block_size))  13.1 us
    unnamed x10, local copies, waits for them, and re-layouts  10.3 us
    dot_general x1, matrix products, on_device(): jnp.einsum('qf,cf->qc', prepared, chosen, preferred_element_type=jnp.floa...  7.78 us
  transfers between devices with their start and end apart: 1, of which 1 were waited for; matrix products, arithmetic and copies ran while one was open for 21% of the time, Pallas kernels for 0%

commit v1 on v0

--- a/solution.py
+++ b/solution.py
@@ -1,7 +1,65 @@
 import jax
 import jax.numpy as jnp
 from jax import lax
+from jax.experimental import pallas as pl
+from jax.experimental.pallas import tpu as pltpu
 from jax.sharding import PartitionSpec as P
+
+LANES = 128
+
+
+def gather_kernel(ids_ref, table_ref, out_ref):
+    ids = ids_ref[0]
+    docs, entries = table_ref.shape[1], ids.shape[1]
+    group, row = ids // LANES, ids % LANES
+    in_group = (lax.broadcasted_iota(jnp.int32, (LANES, entries), 0) == row).astype(jnp.bfloat16)
+    one_hot = jnp.concatenate(
+        [in_group * (group == g).astype(jnp.bfloat16) for g in range(docs // LANES)], axis=0
+    )
+    out_ref[0] = jnp.dot(table_ref[...], one_hot, preferred_element_type=jnp.float32).astype(
+        out_ref.dtype
+    )
+
+
+def gather_columns(ids, table):
+    batches, _, entries = ids.shape
+    features, docs = table.shape
+    return pl.pallas_call(
+        gather_kernel,
+        grid=(batches,),
+        in_specs=[
+            pl.BlockSpec((1, 1, entries), lambda b: (b, 0, 0)),
+            pl.BlockSpec((features, docs), lambda b: (0, 0)),
+        ],
+        out_specs=pl.BlockSpec((1, features, entries), lambda b: (b, 0, 0)),
+        out_shape=jax.ShapeDtypeStruct((batches, features, entries), table.dtype),
+        compiler_params=pltpu.CompilerParams(vmem_limit_bytes=48 << 20),
+        cost_estimate=pl.CostEstimate(
+            flops=2 * batches * features * docs * entries,
+            bytes_accessed=2 * features * (docs + batches * entries),
+            transcendentals=0,
+        ),
+    )(ids, table)
+
+
+def score_kernel(scale, prepared_ref, chosen_ref, total_ref, out_ref):
+    part = jnp.dot(prepared_ref[...], chosen_ref[...], preferred_element_type=jnp.float32)
+    out_ref[...] = (total_ref[...] + part) * scale
+
+
+def add_scores(prepared, chosen, total, scale):
+    return pl.pallas_call(
+        lambda *refs: score_kernel(scale, *refs),
+        in_specs=[pl.BlockSpec(memory_space=pltpu.VMEM)] * 3,
+        out_specs=pl.BlockSpec(memory_space=pltpu.VMEM),
+        out_shape=jax.ShapeDtypeStruct(total.shape, total.dtype),
+        compiler_params=pltpu.CompilerParams(vmem_limit_bytes=48 << 20),
+        cost_estimate=pl.CostEstimate(
+            flops=2 * prepared.shape[0] * prepared.shape[1] * chosen.shape[1],
+            bytes_accessed=2 * prepared.size + 2 * chosen.size + 8 * total.size,
+            transcendentals=0,
+        ),
+    )(prepared, chosen, total)
 
 
 def precondition(queries, left_inv, right_inv):
@@ -24,21 +82,42 @@
     return jnp.concatenate(pieces, axis=1)
 
 
+def chunks_of(width):
+    if width % 512:
+        return [(0, width)]
+    quarter = width // 4
+    return [(0, quarter), (2 * quarter, 2 * quarter), (quarter, quarter)]
+
+
 def on_device(doc_grads, query_grads, left_inv, right_inv, cand_owner, cand_row):
     devices = lax.axis_size("docs")
     doc_count = doc_grads.shape[0] // devices
-    requests = cand_row.shape[0]
-    owners = cand_owner[:, 0]
-    every_owner, every_row = (
-        lax.all_gather(owners, "docs", axis=0, tiled=True),
-        lax.all_gather(cand_row, "docs", axis=0, tiled=True),
+    entries = cand_row.shape[0]
+    width = doc_grads.shape[1]
+    queries = query_grads.shape[0]
+    own_ids = cand_owner[:, 0] * doc_count + cand_row
+    ids = lax.all_to_all(
+        jnp.broadcast_to(own_ids, (devices, 1, entries)), "docs", split_axis=0, concat_axis=0, tiled=True
     )
-    doc_ids = (every_owner * doc_count + every_row).reshape(devices, requests)
-    pieces = jnp.take(doc_grads, doc_ids, axis=0)
-    chosen = lax.all_to_all(pieces, "docs", split_axis=0, concat_axis=2, tiled=True)[0]
-    prepared = precondition(query_grads, left_inv, right_inv)
-    scores = jnp.einsum("qf,cf->qc", prepared, chosen, preferred_element_type=jnp.float32)
-    return scores * prepared.shape[1] ** (-0.5)
+    table = doc_grads.T
+    chosen = []
+    for start, size in chunks_of(width):
+        piece = gather_columns(ids, table[start : start + size])
+        ids, _ = lax.optimization_barrier((ids, piece))
+        chosen.append(
+            lax.all_to_all(piece, "docs", split_axis=0, concat_axis=0, tiled=True).reshape(
+                devices * size, entries
+            )
+        )
+    prepared = precondition(query_grads, left_inv, right_inv).reshape(queries, devices, width)
+    scores = jnp.zeros((queries, entries), jnp.float32)
+    for i, (start, size) in enumerate(chunks_of(width)):
+        block = prepared[:, :, start : start + size].reshape(queries, devices * size)
+        last = i == len(chosen) - 1
+        scores = add_scores(
+            block, chosen[i], scores, query_grads.shape[1] ** (-0.5) if last else 1.0
+        )
+    return scores
 
 
 def solution(mesh):

time: 174 us -> 174 us (level)
  the two profiles are of different devices: /device:TPU:15 before, /device:TPU:0 now
where the time goes in v1:
time: 174 us; the launch traced here: 173 us
  local copies, waits for them, and re-layouts  52.2 us (30%)
  waiting for transfers between devices  49.1 us (28%)
  starting transfers between devices  29.5 us (17%)
  Pallas kernels  27.7 us (16%)
  matrix products  13.2 us (8%)
    all_to_all x3, waiting for transfers between devices, on_device(): lax.all_to_all(piece, 'docs', split_axis=0, concat_axis=0, tiled=True)  46.6 us
    unnamed x24, local copies, waits for them, and re-layouts  31.8 us
    all_to_all x3, starting transfers between devices, on_device(): lax.all_to_all(piece, 'docs', split_axis=0, concat_axis=0, tiled=True)  22.1 us
    pallas_call x3, Pallas kernels, gather_columns(): pl.pallas_call(gather_kernel, grid=(batches,), in_specs=[pl.BlockSpec((1,...  20.8 us
    concatenate x3, local copies, waits for them, and re-layouts, precondition(): return jnp.concatenate(pieces, axis=1)  16.2 us
    dot_general x2, matrix products, precondition(): jnp.einsum('ai,qik->qak', left_inv[layer_index], middle, preferred_elemen...  13.2 us
    all_to_all x1, starting transfers between devices, on_device(): lax.all_to_all(jnp.broadcast_to(own_ids, (devices, 1, entries)), 'docs',...  7.39 us
    pallas_call x3, Pallas kernels, add_scores(): pl.pallas_call(lambda *refs: score_kernel(scale, *refs), in_specs=[pl.Blo...  6.88 us
  transfers between devices with their start and end apart: 4, of which 3 were waited for; matrix products, arithmetic and copies ran while one was open for 34% of the time, Pallas kernels for 10%

profile of v1, /device:TPU:0, one launch (start us, length us, event | category | flops | bytes accessed | tf_op | source)
XLA Modules:
  0.0 173.2 jit_solution(3784834802512305987)
XLA Ops:
  0.0 0.7 broadcast_multiply_fusion
  0.7 0.7 add.3
  1.4 0.6 broadcast_in_dim.6
  2.0 7.4 %all-to-all-start = ((s32[16,1,256]{2,1,0:T(1,128)}), s32[16,1,256]{2,1,0:T(1,128)S(1)}, u32[]{:S(2)}, u32[]{:S(2)}) async-start(s32[16,1,256]{2,1,0:T(1,128)} %broadcast_in_dim.6), calls=%async_computation | async-start | bytes 32768 | tf_op jit(solution)/shard_map/all_to_all | solution.py:99
  9.4 2.9 %copy.7 = bf16[2048,512]{0,1:T(8,128)(2,1)S(1)} copy(bf16[2048,512]{1,0:T(8,128)(2,1)} %param.6) | data formatting | bytes 4194304 | tf_op args[0]
  12.3 0.0 copy-start.5
  12.3 1.0 fusion.25
  13.3 2.5 %all-to-all-done.ids_ref = s32[16,1,256]{2,1,0:T(1,128)S(1)} async-done(((s32[16,1,256]{2,1,0:T(1,128)}), s32[16,1,256]{2,1,0:T(1,128)S(1)}, u32[]{:S(2)}, u32[]{:S(2)}) %all-to-all-start) | async-done | bytes 16416 | tf_op jit(solution)/shard_map/all_to_all | solution.py:99
  15.9 0.0 copy-done.5
  15.9 8.0 %shard_map.64 = bf16[16,128,256]{2,1,0:T(8,128)(2,1)} custom-call(s32[16,1,256]{2,1,0:T(1,128)S(1)} %all-to-all-done.ids_ref, bf16[128,2048]{1,0:T(8,128)(2,1)S(1)} %get-tuple-element.14.table_ref), custom_call_target="tpu_custom_call" | custom-call | flops 2147483648 | bytes 1572864 | tf_op jit(solution)/shard_map/pallas_call | solution.py:27
  23.9 3.9 %all-to-all-start.3 = ((bf16[16,128,256]{2,1,0:T(8,128)(2,1)}), bf16[16,128,256]{2,1,0:T(8,128)(2,1)S(1)}, u32[]{:S(2)}, u32[]{:S(2)}) async-start(bf16[16,128,256]{2,1,0:T(8,128)(2,1)} %shard_map.64), calls=%async_computation.3 | async-start | bytes 2097152 | tf_op jit(solution)/shard_map/all_to_all | solution.py:108
  27.9 1.3 slice.50.table_ref
  29.2 7.4 %shard_map.65 = bf16[16,256,256]{2,1,0:T(8,128)(2,1)S(1)} custom-call(s32[16,1,256]{2,1,0:T(1,128)S(1)} %all-to-all-done.ids_ref, bf16[256,2048]{1,0:T(8,128)(2,1)S(1)} %slice.50.table_ref), custom_call_target="tpu_custom_call" | custom-call | flops 4294967296 | bytes 3145728 | tf_op jit(solution)/shard_map/pallas_call | solution.py:27
  36.6 0.0 copy-start.1
  36.6 1.3 copy-done.1
  37.9 12.9 %all-to-all-done.3 = bf16[16,128,256]{2,1,0:T(8,128)(2,1)S(1)} async-done(((bf16[16,128,256]{2,1,0:T(8,128)(2,1)}), bf16[16,128,256]{2,1,0:T(8,128)(2,1)S(1)}, u32[]{:S(2)}, u32[]{:S(2)}) %all-to-all-start.3) | async-done | bytes 1048608 | tf_op jit(solution)/shard_map/all_to_all | solution.py:108
  50.8 6.9 %all-to-all-start.2 = ((bf16[16,256,256]{2,1,0:T(8,128)(2,1)}), bf16[16,256,256]{2,1,0:T(8,128)(2,1)S(1)}, u32[]{:S(2)}, u32[]{:S(2)}) async-start(bf16[16,256,256]{2,1,0:T(8,128)(2,1)} %copy-done.1), calls=%async_computation.2 | async-start | bytes 4194304 | tf_op jit(solution)/shard_map/all_to_all | solution.py:108
  57.7 0.0 copy-start.3
  57.7 1.0 copy-done.3
  58.7 5.4 %shard_map.66 = bf16[16,128,256]{2,1,0:T(8,128)(2,1)S(1)} custom-call(s32[16,1,256]{2,1,0:T(1,128)S(1)} %all-to-all-done.ids_ref, bf16[128,2048]{1,0:T(8,128)(2,1)S(1)} %copy-done.3), custom_call_target="tpu_custom_call" | custom-call | flops 2147483648 | bytes 1572864 | tf_op jit(solution)/shard_map/pallas_call | solution.py:27
  64.1 0.0 copy-start.2
  64.1 1.0 copy-done.2
  65.1 33.7 %all-to-all-done.2 = bf16[16,256,256]{2,1,0:T(8,128)(2,1)S(1)} async-done(((bf16[16,256,256]{2,1,0:T(8,128)(2,1)}), bf16[16,256,256]{2,1,0:T(8,128)(2,1)S(1)}, u32[]{:S(2)}, u32[]{:S(2)}) %all-to-all-start.2) | async-done | bytes 2097184 | tf_op jit(solution)/shard_map/all_to_all | solution.py:108
  98.8 11.3 %all-to-all-start.1 = ((bf16[16,128,256]{2,1,0:T(8,128)(2,1)}), bf16[16,128,256]{2,1,0:T(8,128)(2,1)}, u32[]{:S(2)}, u32[]{:S(2)}) async-start(bf16[16,128,256]{2,1,0:T(8,128)(2,1)} %copy-done.2), calls=%async_computation.1 | async-start | bytes 2097152 | tf_op jit(solution)/shard_map/all_to_all | solution.py:108
  110.1 5.2 %slice_bitcast_fusion = (bf16[64,8,32,128]{3,1,2,0:T(8,128)(2,1)}, bf16[64,8,32,128]{3,1,2,0:T(8,128)(2,1)S(1)}) fusion(bf16[512,8192]{1,0:T(8,128)(2,1)} %param.7), kind=kLoop, calls=%fused_computation.3 | loop fusion | bytes 16777216
  115.3 0.0 copy-start.6
  115.3 0.0 copy-start.7
  115.3 3.2 %copy.8 = bf16[64,8,32,128]{3,2,1,0:T(8,128)(2,1)} copy(bf16[64,8,32,128]{3,1,2,0:T(8,128)(2,1)S(1)} %get-tuple-element.12) | data formatting | bytes 8388608
  118.5 0.0 copy-done.6
  118.5 0.0 copy-done.7
  118.5 6.6 %convert_bitcast_fusion.1 = bf16[512,32,128]{2,1,0:T(8,128)(2,1)} fusion(bf16[512,32,128]{2,1,0:T(8,128)(2,1)} %bitcast.50, bf16[2,128,128]{2,1,0:T(8,128)(2,1)S(1)} %copy-done.6, bf16[2,32,32]{2,1,0:T(8,128)(2,1)S(1)} %copy-done.7), kind=kOutput, calls=%fused_computation.4 | convolution fusion | flops 675282944 | bytes 8429568 | tf_op jit(solution)/shard_map/ai,qik->qak/dot_general | solution.py:78
  125.1 7.5 %concatenate.8 = bf16[512,8,512]{2,1,0:T(8,128)(2,1)} reshape(bf16[512,32,128]{2,1,0:T(8,128)(2,1)} %convert_bitcast_fusion.1) | data formatting | bytes 8388608 | tf_op jit(solution)/shard_map/concatenate | solution.py:82
  132.6 5.4 %copy.9 = bf16[64,8,32,128]{3,2,1,0:T(8,128)(2,1)} copy(bf16[64,8,32,128]{3,1,2,0:T(8,128)(2,1)} %get-tuple-element.11) | data formatting | bytes 8388608
  138.1 6.6 %convert_bitcast_fusion = bf16[512,32,128]{2,1,0:T(8,128)(2,1)} fusion(bf16[512,32,128]{2,1,0:T(8,128)(2,1)} %bitcast.51, bf16[2,128,128]{2,1,0:T(8,128)(2,1)S(1)} %copy-done.6, bf16[2,32,32]{2,1,0:T(8,128)(2,1)S(1)} %copy-done.7), kind=kOutput, calls=%fused_computation | convolution fusion | flops 675282944 | bytes 8429568 | tf_op jit(solution)/shard_map/ai,qik->qak/dot_general | solution.py:78
  144.7 7.6 %concatenate.9 = bf16[512,8,512]{2,1,0:T(8,128)(2,1)} reshape(bf16[512,32,128]{2,1,0:T(8,128)(2,1)} %convert_bitcast_fusion) | data formatting | bytes 8388608 | tf_op jit(solution)/shard_map/concatenate | solution.py:82
  152.3 0.0 copy-start.4
  152.3 3.0 %constant_dynamic-update-slice_fusion.1 = bf16[512,16,512]{2,1,0:T(8,128)(2,1)S(1)} fusion(bf16[512,8,512]{2,1,0:T(8,128)(2,1)} %concatenate.8), kind=kLoop, calls=%fused_computation.21 | loop fusion | bytes 8388608
  155.3 0.5 copy-done.4
  155.7 1.1 constant_dynamic-update-slice_fusion
  156.8 0.5 slice.52
  157.3 0.7 fusion.24
  158.1 0.5 copy.15
  158.6 4.2 %copy.11 = bf16[64,8,16,256]{3,1,2,0:T(8,128)(2,1)} copy(bf16[64,8,16,256]{3,2,1,0:T(8,128)(2,1)S(1)} %bitcast.52) | data formatting | bytes 8388608
  162.8 1.9 %copy.16 = bf16[64,8,16,128]{3,1,2,0:T(8,128)(2,1)} copy(bf16[64,8,16,128]{3,2,1,0:T(8,128)(2,1)S(1)} %bitcast.55) | data formatting | bytes 4194304
  164.7 0.7 shard_map.67.refs_2_
  165.4 3.4 %shard_map.68.refs_2_ = f32[512,256]{1,0:T(8,128)S(1)} custom-call(bf16[512,4096]{1,0:T(8,128)(2,1)} %bitcast.49, bf16[4096,256]{1,0:T(8,128)(2,1)S(1)} %bitcast.45, f32[512,256]{1,0:T(8,128)S(1)} %shard_map.67.refs_2_), custom_call_target="tpu_custom_call" | custom-call | flops 1073741824 | bytes 7340032 | tf_op jit(solution)/shard_map/pallas_call | solution.py:51
  168.9 0.0 all-to-all-done.1
  168.9 0.0 copy-start
  168.9 1.6 copy-done
  170.5 2.7 %shard_map.69 = f32[512,256]{1,0:T(8,128)} custom-call(bf16[512,2048]{1,0:T(8,128)(2,1)S(1)} %bitcast.46, bf16[2048,256]{1,0:T(8,128)(2,1)} %bitcast.12.refs_1_, f32[512,256]{1,0:T(8,128)S(1)} %shard_map.68.refs_2_), custom_call_target="tpu_custom_call" | custom-call | flops 536870912 | bytes 4194304 | tf_op jit(solution)/shard_map/pallas_call | solution.py:51
  (1 shorter events, 0.0 us)
Async XLA Ops:
  2.0 13.9 %all-to-all-start = ((s32[16,1,256]{2,1,0:T(1,128)}), s32[16,1,256]{2,1,0:T(1,128)S(1)}, u32[]{:S(2)}, u32[]{:S(2)}) async-start(s32[16,1,256]{2,1,0:T(1,128)} %broadcast_in_dim.6), calls=%async_computation | async-start | bytes 32768 | tf_op jit(solution)/shard_map/all_to_all | solution.py:99
  12.3 3.6 %copy-start.5 = (bf16[2048,512]{0,1:T(8,128)(2,1)}, bf16[2048,512]{0,1:T(8,128)(2,1)S(1)}, u32[]{:S(2)}) copy-start(bf16[2048,512]{0,1:T(8,128)(2,1)S(1)} %copy.7) | copy-start | bytes 6291460
  23.9 26.9 %all-to-all-start.3 = ((bf16[16,128,256]{2,1,0:T(8,128)(2,1)}), bf16[16,128,256]{2,1,0:T(8,128)(2,1)S(1)}, u32[]{:S(2)}, u32[]{:S(2)}) async-start(bf16[16,128,256]{2,1,0:T(8,128)(2,1)} %shard_map.64), calls=%async_computation.3 | async-start | bytes 2097152 | tf_op jit(solution)/shard_map/all_to_all | solution.py:108
  36.6 1.3 copy-start.1
  50.8 48.0 %all-to-all-start.2 = ((bf16[16,256,256]{2,1,0:T(8,128)(2,1)}), bf16[16,256,256]{2,1,0:T(8,128)(2,1)S(1)}, u32[]{:S(2)}, u32[]{:S(2)}) async-start(bf16[16,256,256]{2,1,0:T(8,128)(2,1)} %copy-done.1), calls=%async_computation.2 | async-start | bytes 4194304 | tf_op jit(solution)/shard_map/all_to_all | solution.py:108
  57.7 1.0 copy-start.3
  64.1 1.0 copy-start.2
  98.8 70.1 %all-to-all-start.1 = ((bf16[16,128,256]{2,1,0:T(8,128)(2,1)}), bf16[16,128,256]{2,1,0:T(8,128)(2,1)}, u32[]{:S(2)}, u32[]{:S(2)}) async-start(bf16[16,128,256]{2,1,0:T(8,128)(2,1)} %copy-done.2), calls=%async_computation.1 | async-start | bytes 2097152 | tf_op jit(solution)/shard_map/all_to_all | solution.py:108
  115.3 3.2 %copy-start.6 = (bf16[2,128,128]{2,1,0:T(8,128)(2,1)S(1)}, bf16[2,128,128]{2,1,0:T(8,128)(2,1)}, u32[]{:S(2)}) copy-start(bf16[2,128,128]{2,1,0:T(8,128)(2,1)} %param.9) | copy-start | bytes 196612
  115.3 3.2 %copy-start.7 = (bf16[2,32,32]{2,1,0:T(8,128)(2,1)S(1)}, bf16[2,32,32]{2,1,0:T(8,128)(2,1)}, u32[]{:S(2)}) copy-start(bf16[2,32,32]{2,1,0:T(8,128)(2,1)} %param.8) | copy-start | bytes 12292
  152.3 3.4 %copy-start.4 = (bf16[512,8,512]{2,1,0:T(8,128)(2,1)S(1)}, bf16[512,8,512]{2,1,0:T(8,128)(2,1)}, u32[]{:S(2)}) copy-start(bf16[512,8,512]{2,1,0:T(8,128)(2,1)} %concatenate.9) | copy-start | bytes 12582916
  168.9 1.6 copy-start

commit v2 on v0

--- a/solution.py
+++ b/solution.py
@@ -1,7 +1,176 @@
 import jax
 import jax.numpy as jnp
 from jax import lax
+from jax.experimental import pallas as pl
+from jax.experimental.pallas import tpu as pltpu
 from jax.sharding import PartitionSpec as P
+
+LANES = 128
+VMEM_BYTES = 48 << 20
+
+
+def one_hot(ids, docs):
+    group, row = ids // LANES, ids % LANES
+    in_group = (lax.broadcasted_iota(jnp.int32, (LANES, ids.shape[1]), 0) == row).astype(jnp.bfloat16)
+    return jnp.concatenate(
+        [in_group * (group == g).astype(jnp.bfloat16) for g in range(docs // LANES)], axis=0
+    )
+
+
+def gather_all_kernel(ids_ref, table_ref, out_ref):
+    table = table_ref[...]
+    out_ref[0] = jnp.dot(
+        table, one_hot(ids_ref[0], table.shape[1]), preferred_element_type=jnp.float32
+    ).astype(out_ref.dtype)
+
+
+def gather_all(ids, table):
+    batches, _, entries = ids.shape
+    features, docs = table.shape
+    return pl.pallas_call(
+        gather_all_kernel,
+        grid=(batches,),
+        in_specs=[
+            pl.BlockSpec((1, 1, entries), lambda b: (b, 0, 0)),
+            pl.BlockSpec((features, docs), lambda b: (0, 0)),
+        ],
+        out_specs=pl.BlockSpec((1, features, entries), lambda b: (b, 0, 0)),
+        out_shape=jax.ShapeDtypeStruct((batches, features, entries), table.dtype),
+        compiler_params=pltpu.CompilerParams(vmem_limit_bytes=VMEM_BYTES),
+        cost_estimate=pl.CostEstimate(
+            flops=2 * batches * features * docs * entries,
+            bytes_accessed=2 * features * (docs + batches * entries),
+            transcendentals=0,
+        ),
+    )(ids, table)
+
+
+def gather_near_kernel(count, me_ref, *refs):
+    ids_refs, tables, out_refs = refs[:count], refs[count : count + 2], refs[count + 2 :]
+    features, docs = tables[0].shape
+    for ids_ref, out_ref in zip(ids_refs, out_refs):
+        hot = one_hot(ids_ref[0], docs)
+        for i, table_ref in enumerate(tables):
+            out_ref[i * features : (i + 1) * features, :] = jnp.dot(
+                table_ref[...], hot, preferred_element_type=jnp.float32
+            ).astype(out_ref.dtype)
+
+
+def gather_near(me, ids, own, far, partners):
+    entries = ids.shape[2]
+    features, docs = own.shape
+    count = len(partners)
+    return pl.pallas_call(
+        lambda *refs: gather_near_kernel(count, *refs),
+        grid_spec=pltpu.PrefetchScalarGridSpec(
+            num_scalar_prefetch=1,
+            grid=(1,),
+            in_specs=[
+                pl.BlockSpec((1, 1, entries), lambda i, me, k=k: (me[0] ^ k, 0, 0)) for k in partners
+            ]
+            + [pl.BlockSpec((features, docs), lambda i, me: (0, 0))] * 2,
+            out_specs=[pl.BlockSpec((2 * features, entries), lambda i, me: (0, 0))] * count,
+        ),
+        out_shape=[jax.ShapeDtypeStruct((2 * features, entries), own.dtype)] * count,
+        compiler_params=pltpu.CompilerParams(vmem_limit_bytes=VMEM_BYTES),
+        cost_estimate=pl.CostEstimate(
+            flops=4 * count * features * docs * entries,
+            bytes_accessed=4 * features * (docs + count * entries),
+            transcendentals=0,
+        ),
+    )(me, *[ids] * count, own, far)
+
+
+def score_near_kernel(count, me_ref, *refs):
+    own_refs, far_refs, chosen_refs, out_ref = (
+        refs[:count],
+        refs[count : 2 * count],
+        refs[2 * count : 3 * count],
+        refs[-1],
+    )
+    total = None
+    for own, far, chosen in zip(own_refs, far_refs, chosen_refs):
+        pair = jnp.concatenate([own[...], far[...]], axis=1)
+        part = jnp.dot(pair, chosen[...], preferred_element_type=jnp.float32)
+        total = part if total is None else total + part
+    out_ref[...] = total
+
+
+def score_near(me, prepared, chosen, partners, half, width):
+    queries = prepared.shape[0]
+    features, entries = chosen[0].shape
+    size = features // 2
+    stride = width // size
+    count = len(partners)
+    return pl.pallas_call(
+        lambda *refs: score_near_kernel(count, *refs),
+        grid_spec=pltpu.PrefetchScalarGridSpec(
+            num_scalar_prefetch=1,
+            grid=(1,),
+            in_specs=[
+                pl.BlockSpec((queries, size), lambda i, me, k=k: (0, (me[0] ^ k) * stride))
+                for k in list(partners) + [k ^ half for k in partners]
+            ]
+            + [pl.BlockSpec((features, entries), lambda i, me: (0, 0))] * count,
+            out_specs=pl.BlockSpec((queries, entries), lambda i, me: (0, 0)),
+        ),
+        out_shape=jax.ShapeDtypeStruct((queries, entries), jnp.float32),
+        compiler_params=pltpu.CompilerParams(vmem_limit_bytes=VMEM_BYTES),
+        cost_estimate=pl.CostEstimate(
+            flops=2 * count * queries * features * entries,
+            bytes_accessed=2 * count * features * (queries + entries) + 4 * queries * entries,
+            transcendentals=0,
+        ),
+    )(me, *[prepared] * (2 * count), *chosen)
+
+
+def score_all_kernel(width, scale, prepared_ref, chosen_ref, total_ref, out_ref):
+    sources, features, _ = chosen_ref.shape
+    step = pl.program_id(0)
+    part = sum(
+        jnp.dot(
+            prepared_ref[:, s * width + width - features : (s + 1) * width],
+            chosen_ref[s],
+            preferred_element_type=jnp.float32,
+        )
+        for s in range(sources)
+    )
+
+    @pl.when(step == 0)
+    def _():
+        out_ref[...] = total_ref[...] + part
+
+    @pl.when(step > 0)
+    def _():
+        out_ref[...] += part
+
+    @pl.when(step == pl.num_programs(0) - 1)
+    def _():
+        out_ref[...] *= scale
+
+
+def score_all(prepared, chosen, total, width, scale):
+    queries = prepared.shape[0]
+    devices, features, entries = chosen.shape
+    steps = 4
+    whole = pl.BlockSpec((queries, entries), lambda i: (0, 0))
+    return pl.pallas_call(
+        lambda *refs: score_all_kernel(width, scale, *refs),
+        grid=(steps,),
+        in_specs=[
+            pl.BlockSpec((queries, devices // steps * width), lambda i: (0, i)),
+            pl.BlockSpec((devices // steps, features, entries), lambda i: (i, 0, 0)),
+            whole,
+        ],
+        out_specs=whole,
+        out_shape=jax.ShapeDtypeStruct((queries, entries), jnp.float32),
+        compiler_params=pltpu.CompilerParams(vmem_limit_bytes=VMEM_BYTES),
+        cost_estimate=pl.CostEstimate(
+            flops=2 * devices * features * queries * entries,
+            bytes_accessed=2 * devices * features * (queries + entries) + 8 * queries * entries,
+            transcendentals=0,
+        ),
+    )(prepared, chosen, total)
 
 
 def precondition(queries, left_inv, right_inv):
@@ -26,19 +195,38 @@
 
 def on_device(doc_grads, query_grads, left_inv, right_inv, cand_owner, cand_row):
     devices = lax.axis_size("docs")
+    half = devices // 2
     doc_count = doc_grads.shape[0] // devices
-    requests = cand_row.shape[0]
-    owners = cand_owner[:, 0]
-    every_owner, every_row = (
-        lax.all_gather(owners, "docs", axis=0, tiled=True),
-        lax.all_gather(cand_row, "docs", axis=0, tiled=True),
-    )
-    doc_ids = (every_owner * doc_count + every_row).reshape(devices, requests)
-    pieces = jnp.take(doc_grads, doc_ids, axis=0)
-    chosen = lax.all_to_all(pieces, "docs", split_axis=0, concat_axis=2, tiled=True)[0]
+    entries = cand_row.shape[0]
+    width = doc_grads.shape[1]
+    queries, features = query_grads.shape
+
+    def swap(values, k):
+        return lax.ppermute(values, "docs", [(i, i ^ k) for i in range(devices)])
+
+    head = width // 4 if width % (4 * LANES) == 0 else 0
+    if head:
+        own = doc_grads[:, :head].T
+        far = swap(own, half)
+    own_ids = cand_owner[:, 0] * doc_count + cand_row
+    ids = lax.all_to_all(
+        jnp.broadcast_to(own_ids, (devices, 1, entries)), "docs", split_axis=0, concat_axis=0, tiled=True
+    )
+    picked = gather_all(ids, doc_grads[:, head:].T)
+    ids, query_grads, picked = lax.optimization_barrier((ids, query_grads, picked))
+    chosen = lax.all_to_all(picked, "docs", split_axis=0, concat_axis=0, tiled=True)
+    if head:
+        me = lax.axis_index("docs").astype(jnp.int32).reshape(1)
+        partners = list(range(half))
+        pieces = gather_near(me, ids, own, far, partners)
+        query_grads, pieces = lax.optimization_barrier((query_grads, pieces))
+        near = [piece if k == 0 else swap(piece, k) for k, piece in zip(partners, pieces)]
     prepared = precondition(query_grads, left_inv, right_inv)
-    scores = jnp.einsum("qf,cf->qc", prepared, chosen, preferred_element_type=jnp.float32)
-    return scores * prepared.shape[1] ** (-0.5)
+    if head:
+        total = score_near(me, prepared, near, partners, half, width)
+    else:
+        total = jnp.zeros((queries, entries), jnp.float32)
+    return score_all(prepared, chosen, total, width, features ** (-0.5))
 
 
 def solution(mesh):

time: 174 us -> 190 us (1.092)
  the two profiles are of different devices: /device:TPU:15 before, /device:TPU:0 now
where the time goes in v2:
time: 190 us; the launch traced here: 189 us
  waiting for transfers between devices  92.3 us (49%)
  local copies, waits for them, and re-layouts  39.3 us (21%)
  Pallas kernels  22.6 us (12%)
  starting transfers between devices  20.1 us (11%)
  matrix products  13.2 us (7%)
    ppermute x8, waiting for transfers between devices, swap(): return lax.ppermute(values, 'docs', [(i, i ^ k) for i in range(devices)])  87.4 us
    unnamed x22, local copies, waits for them, and re-layouts  28.3 us
    dot_general x2, matrix products, precondition(): jnp.einsum('ai,qik->qak', left_inv[layer_index], middle, preferred_elemen...  13.2 us
    pallas_call x1, Pallas kernels, gather_all(): pl.pallas_call(gather_all_kernel, grid=(batches,), in_specs=[pl.BlockSpec...  9.54 us
    ppermute x8, starting transfers between devices, swap(): return lax.ppermute(values, 'docs', [(i, i ^ k) for i in range(devices)])  9.02 us
    concatenate x1, local copies, waits for them, and re-layouts, precondition(): return jnp.concatenate(pieces, axis=1)  8.54 us
    all_to_all x1, starting transfers between devices, on_device(): lax.all_to_all(jnp.broadcast_to(own_ids, (devices, 1, entries)), 'docs',...  7.39 us
    pallas_call x1, Pallas kernels, score_all(): pl.pallas_call(lambda *refs: score_all_kernel(width, scale, *refs), grid=...  6.45 us
  transfers between devices with their start and end apart: 10, of which 2 were waited for; matrix products, arithmetic and copies ran while one was open for 24% of the time, Pallas kernels for 3%

profile of v2, /device:TPU:0, one launch (start us, length us, event | category | flops | bytes accessed | tf_op | source)
XLA Modules:
  0.0 189.1 jit_solution(2237599616291765215)
XLA Ops:
  0.0 0.0 slice-start
  0.0 0.8 broadcast_multiply_fusion
  0.8 0.7 add.3
  1.5 0.6 broadcast_in_dim.3
  2.1 7.4 %all-to-all-start = ((s32[16,1,256]{2,1,0:T(1,128)}), s32[16,1,256]{2,1,0:T(1,128)S(1)}, u32[]{:S(2)}, u32[]{:S(2)}) async-start(s32[16,1,256]{2,1,0:T(1,128)} %broadcast_in_dim.3), calls=%async_computation | async-start | bytes 32768 | tf_op jit(solution)/shard_map/all_to_all | solution.py:212
  9.5 0.0 slice-done
  9.5 1.6 copy.9
  11.2 4.8 %all-to-all-done.ids_ref.refs_1_.refs_2_.refs_3_.refs_4_.refs_5_.refs_6_.refs_7_.refs_8_ = s32[16,1,256]{2,1,0:T(1,128)S(1)} async-done(((s32[16,1,256]{2,1,0:T(1,128)}), s32[16,1,256]{2,1,0:T(1,128)S(1)}, u32[]{:S(2)}, u32[]{:S(2)}) %all-to-all-start) | async-done | bytes 16416 | tf_op jit(solution)/shard_map/all_to_all | solution.py:212
  16.0 0.0 copy-start.3
  16.0 1.4 copy-done.3
  17.4 9.5 %shard_map.64 = bf16[16,384,256]{2,1,0:T(8,128)(2,1)S(1)} custom-call(s32[16,1,256]{2,1,0:T(1,128)S(1)} %all-to-all-done.ids_ref.refs_1_.refs_2_.refs_3_.refs_4_.refs_5_.refs_6_.refs_7_.refs_8_, bf16[384,2048]{1,0:T(8,128)(2,1)S(1)} %bitcast.38), custom_call_target="tpu_custom_call" | custom-call | flops 6442450944 | bytes 4718592 | tf_op jit(solution)/shard_map/pallas_call | solution.py:30
  27.0 0.0 copy-start
  27.0 1.6 copy-done
  28.6 3.7 %all-to-all-start.1 = ((bf16[16,384,256]{2,1,0:T(8,128)(2,1)}), bf16[16,384,256]{2,1,0:T(8,128)(2,1)S(1)}, u32[]{:S(2)}, u32[]{:S(2)}) async-start(bf16[16,384,256]{2,1,0:T(8,128)(2,1)} %copy-done), calls=%async_computation.1 | async-start | bytes 6291456 | tf_op jit(solution)/shard_map/all_to_all | solution.py:217
  32.3 1.9 slice.25
  34.2 2.0 %copy.10 = bf16[2048,128]{0,1:T(8,128)(2,1)} copy(bf16[2048,128]{1,0:T(8,128)(2,1)} %slice.25) | data formatting | bytes 1048576
  36.3 2.8 %collective-permute-start = (bf16[128,2048]{1,0:T(8,128)(2,1)}, bf16[128,2048]{1,0:T(8,128)(2,1)}, u32[]{:S(2)}, u32[]{:S(2)}) collective-permute-start(bf16[128,2048]{1,0:T(8,128)(2,1)} %bitcast.39), channel_id=1, source_target_pairs={{0,8},{1,9},{2,10},{3,11},{4,12},{5,13},{6,14},{7,15},{8,0},{9,1},... | collective-permute-start | bytes 1572872 | tf_op jit(solution)/shard_map/ppermute | solution.py:205
  39.0 87.4 %collective-permute-done.refs_10_ = bf16[128,2048]{1,0:T(8,128)(2,1)} collective-permute-done((bf16[128,2048]{1,0:T(8,128)(2,1)}, bf16[128,2048]{1,0:T(8,128)(2,1)}, u32[]{:S(2)}, u32[]{:S(2)}) %collective-permute-start) | collective-permute-done | bytes 524320 | tf_op jit(solution)/shard_map/ppermute | solution.py:205
  126.4 0.0 copy-start.4
  126.4 1.0 copy-done.4
  127.5 4.1 %shard_map.65 = (bf16[256,256]{1,0:T(8,128)(2,1)S(1)}, bf16[256,256]{1,0:T(8,128)(2,1)}, bf16[256,256]{1,0:T(8,128)(2,1)}, bf16[256,256]{1,0:T(8,128)(2,1)}, bf1...) custom-call(s32[1]{0:T(128)} %bitcast.2.refs_0_, ...), custom_call_target="tpu_custom_call" | custom-call | flops 2147483648 | bytes 2097152 | tf_op jit(solution)/shard_map/pallas_call | solution.py:63
  131.5 0.0 copy-start.5
  131.5 0.0 copy-start.6
  131.5 0.0 collective-permute-start.1
  131.6 1.5 collective-permute-start.2
  133.1 0.3 collective-permute-start.3
  133.4 0.0 collective-permute-start.4
  133.4 1.7 collective-permute-start.5
  135.1 4.0 %slice_bitcast_fusion = (bf16[64,8,32,128]{3,1,2,0:T(8,128)(2,1)S(1)}, bf16[64,8,32,128]{3,1,2,0:T(8,128)(2,1)S(1)}) fusion(bf16[512,8192]{1,0:T(8,128)(2,1)} %param.7), kind=kLoop, calls=%fused_computation.4 | loop fusion | bytes 16777216
  139.1 0.0 copy-done.5
  139.1 0.0 copy-done.6
  139.1 3.2 %copy.13 = bf16[64,8,32,128]{3,2,1,0:T(8,128)(2,1)} copy(bf16[64,8,32,128]{3,1,2,0:T(8,128)(2,1)S(1)} %get-tuple-element.45) | data formatting | bytes 8388608
  142.4 0.0 copy-start.7
  142.4 3.2 %copy.11 = bf16[64,8,32,128]{3,2,1,0:T(8,128)(2,1)} copy(bf16[64,8,32,128]{3,1,2,0:T(8,128)(2,1)S(1)} %get-tuple-element.46) | data formatting | bytes 8388608
  145.6 0.0 copy-done.7
  145.6 6.6 %fusion.8 = bf16[512,128,32]{1,2,0:T(8,128)(2,1)} fusion(bf16[512,32,128]{2,1,0:T(8,128)(2,1)} %bitcast.43, bf16[2,128,128]{2,1,0:T(8,128)(2,1)} %param.9, bf16[2,32,32]{2,1,0:T(8,128)(2,1)S(1)} %copy-done.7), kind=kOutput, calls=%fused_computation.10 | convolution fusion | flops 675282944 | bytes 8429568 | tf_op jit(solution)/shard_map/ai,qik->qak/dot_general | solution.py:189
  152.2 8.3 %bitcast_dynamic-update-slice_fusion.1 = bf16[512,8192]{1,0:T(8,128)(2,1)} fusion(bf16[64,8,32,128]{3,2,1,0:T(8,128)(2,1)} %bitcast.44), kind=kLoop, calls=%fused_computation.1 | loop fusion | bytes 8388608
  160.4 6.6 %fusion.11 = bf16[512,128,32]{1,2,0:T(8,128)(2,1)} fusion(bf16[512,32,128]{2,1,0:T(8,128)(2,1)} %bitcast.42, bf16[2,128,128]{2,1,0:T(8,128)(2,1)} %param.9, bf16[2,32,32]{2,1,0:T(8,128)(2,1)S(1)} %copy-done.7), kind=kOutput, calls=%fused_computation.11 | convolution fusion | flops 675282944 | bytes 8429568 | tf_op jit(solution)/shard_map/ai,qik->qak/dot_general | solution.py:189
  167.0 0.0 collective-permute-done.1.refs_18_
  167.0 1.2 collective-permute-start.6
  168.3 0.0 collective-permute-done.2.refs_19_
  168.3 1.5 collective-permute-start.7
  169.7 8.5 %bitcast_dynamic-update-slice_fusion.refs_1_.refs_2_.refs_3_.refs_4_.refs_5_.refs_6_.refs_7_.refs_8_.refs_9_.refs_10_.refs_11_.refs_12_.refs_13_.refs_14_.refs_15_.refs_16_.refs_0_ = bf16[512,8192]{1,0:T(8,128)(2,1)} fusion(bf16[512,8192]{1,0:T(8,128)(2,1)} %bitcast_dynamic-update-slice_fusion.1, bf16[64,8,32,128]{3,2,1,0:T(8,128)(2,1)} %bitcast.41), kind=kLoop, calls=%fused_computation | loop fusion | bytes 8388608 | tf_op jit(solution)/shard_map/concatenate | solution.py:193
  178.3 0.0 collective-permute-done.3.refs_20_
  178.3 0.0 collective-permute-done.4.refs_21_
  178.3 0.0 collective-permute-done.5.refs_22_
  178.3 0.0 collective-permute-done.6.refs_23_
  178.3 0.0 collective-permute-done.7.refs_24_
  178.3 2.5 %shard_map.66.refs_2_ = f32[512,256]{1,0:T(8,128)S(1)} custom-call(s32[1]{0:T(128)} %bitcast.2.refs_0_, bf16[512,8192]{1,0:T(8,128)(2,1)} %bitcast_dynamic-update-slice_fusion.refs_1_.refs_2_.refs_3_.refs_4_.refs_5_.refs_6_.refs_7_.refs_8_.refs_9_.refs_10_.refs_11_.refs_12_.refs_13_.refs_14_.refs_15_.refs_16_.refs_0_, ...), custom_call_target="tpu_custom_call" | custom-call | flops 536870912 | bytes 3670016 | tf_op jit(solution)/shard_map/pallas_call | solution.py:105
  180.8 0.0 copy-start.1
  180.8 0.8 copy-done.1
  181.6 0.0 all-to-all-done.1.refs_1_
  181.6 0.0 copy-start.2
  181.6 1.0 copy-done.2
  182.7 6.4 %shard_map.67 = f32[512,256]{1,0:T(8,128)} custom-call(bf16[512,8192]{1,0:T(8,128)(2,1)} %bitcast_dynamic-update-slice_fusion.refs_1_.refs_2_.refs_3_.refs_4_.refs_5_.refs_6_.refs_7_.refs_8_.refs_9_.refs_10_.refs_11_.refs_12_.refs_13_.refs_14_.refs_15_.refs_16_.refs_0_, bf16[16,384,256]{2,1,0:T(8,128)(2,1)S(1)} %all-to-all-done.1.refs_1_, ...), custom_call_target="tpu_custom_call" | custom-call | flops 1610612736 | bytes 10485760 | tf_op jit(solution)/shard_map/pallas_call | solution.py:157
Async XLA Ops:
  0.0 9.5 %slice-start = ((bf16[2048,512]{1,0:T(8,128)(2,1)}), bf16[2048,384]{1,0:T(8,128)(2,1)S(1)}, s32[]{:S(2)}) async-start(bf16[2048,512]{1,0:T(8,128)(2,1)} %param.6), calls=%async_computation.2 | async-start | bytes 3145728 | tf_op jit(solution)/shard_map/slice | solution.py:215
  2.1 13.9 %all-to-all-start = ((s32[16,1,256]{2,1,0:T(1,128)}), s32[16,1,256]{2,1,0:T(1,128)S(1)}, u32[]{:S(2)}, u32[]{:S(2)}) async-start(s32[16,1,256]{2,1,0:T(1,128)} %broadcast_in_dim.3), calls=%async_computation | async-start | bytes 32768 | tf_op jit(solution)/shard_map/all_to_all | solution.py:212
  16.0 1.4 copy-start.3
  27.0 1.6 copy-start
  28.6 153.0 %all-to-all-start.1 = ((bf16[16,384,256]{2,1,0:T(8,128)(2,1)}), bf16[16,384,256]{2,1,0:T(8,128)(2,1)S(1)}, u32[]{:S(2)}, u32[]{:S(2)}) async-start(bf16[16,384,256]{2,1,0:T(8,128)(2,1)} %copy-done), calls=%async_computation.1 | async-start | bytes 6291456 | tf_op jit(solution)/shard_map/all_to_all | solution.py:217
  36.3 90.2 %collective-permute-start = (bf16[128,2048]{1,0:T(8,128)(2,1)}, bf16[128,2048]{1,0:T(8,128)(2,1)}, u32[]{:S(2)}, u32[]{:S(2)}) collective-permute-start(bf16[128,2048]{1,0:T(8,128)(2,1)} %bitcast.39), channel_id=1, source_target_pairs={{0,8},{1,9},{2,10},{3,11},{4,12},{5,13},{6,14},{7,15},{8,0},{9,1},... | collective-permute-start | bytes 1572872 | tf_op jit(solution)/shard_map/ppermute | solution.py:205
  126.4 1.0 copy-start.4
  131.5 7.6 %copy-start.5 = (bf16[256,256]{1,0:T(8,128)(2,1)}, bf16[256,256]{1,0:T(8,128)(2,1)S(1)}, u32[]{:S(2)}) copy-start(bf16[256,256]{1,0:T(8,128)(2,1)S(1)} %get-tuple-element.44) | copy-start | bytes 393220
  131.5 7.6 %copy-start.6 = (bf16[256,256]{1,0:T(8,128)(2,1)}, bf16[256,256]{1,0:T(8,128)(2,1)S(1)}, u32[]{:S(2)}) copy-start(bf16[256,256]{1,0:T(8,128)(2,1)S(1)} %get-tuple-element.43) | copy-start | bytes 393220
  131.5 35.5 %collective-permute-start.1 = (bf16[256,256]{1,0:T(8,128)(2,1)}, bf16[256,256]{1,0:T(8,128)(2,1)S(1)}, u32[]{:S(2)}, u32[]{:S(2)}) collective-permute-start(bf16[256,256]{1,0:T(8,128)(2,1)} %get-tuple-element.38), channel_id=1, source_target_pairs={{0,1},{1,0},{2,3},{3,2},{4,5},{5,4},{6,7},{7,6},{8,9},{9,8},{10,11... | collective-permute-start | bytes 393224 | tf_op jit(solution)/shard_map/ppermute | solution.py:205
  131.6 36.7 %collective-permute-start.2 = (bf16[256,256]{1,0:T(8,128)(2,1)}, bf16[256,256]{1,0:T(8,128)(2,1)S(1)}, u32[]{:S(2)}, u32[]{:S(2)}) collective-permute-start(bf16[256,256]{1,0:T(8,128)(2,1)} %get-tuple-element.39), channel_id=1, source_target_pairs={{0,2},{1,3},{2,0},{3,1},{4,6},{5,7},{6,4},{7,5},{8,10},{9,11},{10,... | collective-permute-start | bytes 393224 | tf_op jit(solution)/shard_map/ppermute | solution.py:205
  133.1 45.2 %collective-permute-start.3 = (bf16[256,256]{1,0:T(8,128)(2,1)}, bf16[256,256]{1,0:T(8,128)(2,1)}, u32[]{:S(2)}, u32[]{:S(2)}) collective-permute-start(bf16[256,256]{1,0:T(8,128)(2,1)} %get-tuple-element.40), channel_id=1, source_target_pairs={{0,3},{1,2},{2,1},{3,0},{4,7},{5,6},{6,5},{7,4},{8,11},{9,10},{10,... | collective-permute-start | bytes 393224 | tf_op jit(solution)/shard_map/ppermute | solution.py:205
  133.4 44.9 %collective-permute-start.4 = (bf16[256,256]{1,0:T(8,128)(2,1)}, bf16[256,256]{1,0:T(8,128)(2,1)}, u32[]{:S(2)}, u32[]{:S(2)}) collective-permute-start(bf16[256,256]{1,0:T(8,128)(2,1)} %get-tuple-element.41), channel_id=1, source_target_pairs={{0,4},{1,5},{2,6},{3,7},{4,0},{5,1},{6,2},{7,3},{8,12},{9,13},{10,... | collective-permute-start | bytes 393224 | tf_op jit(solution)/shard_map/ppermute | solution.py:205
  133.4 44.9 %collective-permute-start.5 = (bf16[256,256]{1,0:T(8,128)(2,1)}, bf16[256,256]{1,0:T(8,128)(2,1)}, u32[]{:S(2)}, u32[]{:S(2)}) collective-permute-start(bf16[256,256]{1,0:T(8,128)(2,1)} %get-tuple-element.42), channel_id=1, source_target_pairs={{0,5},{1,4},{2,7},{3,6},{4,1},{5,0},{6,3},{7,2},{8,13},{9,12},{10,... | collective-permute-start | bytes 393224 | tf_op jit(solution)/shard_map/ppermute | solution.py:205
  142.4 3.2 %copy-start.7 = (bf16[2,32,32]{2,1,0:T(8,128)(2,1)S(1)}, bf16[2,32,32]{2,1,0:T(8,128)(2,1)}, u32[]{:S(2)}) copy-start(bf16[2,32,32]{2,1,0:T(8,128)(2,1)} %param.8) | copy-start | bytes 12292
  167.0 11.3 %collective-permute-start.6 = (bf16[256,256]{1,0:T(8,128)(2,1)}, bf16[256,256]{1,0:T(8,128)(2,1)S(1)}, u32[]{:S(2)}, u32[]{:S(2)}) collective-permute-start(bf16[256,256]{1,0:T(8,128)(2,1)} %copy-done.6), channel_id=1, source_target_pairs={{0,6},{1,7},{2,4},{3,5},{4,2},{5,3},{6,0},{7,1},{8,14},{9,15},{10,... | collective-permute-start | bytes 393224 | tf_op jit(solution)/shard_map/ppermute | solution.py:205
  168.3 10.0 %collective-permute-start.7 = (bf16[256,256]{1,0:T(8,128)(2,1)}, bf16[256,256]{1,0:T(8,128)(2,1)S(1)}, u32[]{:S(2)}, u32[]{:S(2)}) collective-permute-start(bf16[256,256]{1,0:T(8,128)(2,1)} %copy-done.5), channel_id=1, source_target_pairs={{0,7},{1,6},{2,5},{3,4},{4,3},{5,2},{6,1},{7,0},{8,15},{9,14},{10,... | collective-permute-start | bytes 393224 | tf_op jit(solution)/shard_map/ppermute | solution.py:205
  180.8 0.8 copy-start.1
  181.6 1.0 copy-start.2

commit v3 on v0

v3 whole, which is shorter than its diff:
```python
import jax
import jax.numpy as jnp
from jax import lax
from jax.experimental import pallas as pl
from jax.experimental.pallas import tpu as pltpu
from jax.sharding import PartitionSpec as P

LANES = 128
SUBLANES = 8
MXU = 256
VMEM_BYTES = 48 << 20


def call(kernel, out_shape, grid, in_specs, out_specs, flops, bytes_accessed, scratch=(), prefetch=0):
    return pl.pallas_call(
        kernel,
        grid_spec=pltpu.PrefetchScalarGridSpec(
            num_scalar_prefetch=prefetch,
            grid=grid,
            in_specs=in_specs,
            out_specs=out_specs,
            scratch_shapes=scratch,
        ),
        out_shape=out_shape,
        compiler_params=pltpu.CompilerParams(vmem_limit_bytes=VMEM_BYTES),
        cost_estimate=pl.CostEstimate(flops=flops, bytes_accessed=bytes_accessed, transcendentals=0),
    )


def dot(a, b):
    return jnp.dot(a, b, preferred_element_type=jnp.float32)


def one_hot(ids, docs):
    group, row = ids // LANES, ids % LANES
    in_group = (lax.broadcasted_iota(jnp.int32, (LANES, ids.shape[1]), 0) == row).astype(jnp.bfloat16)
    return jnp.concatenate(
        [in_group * (group == g).astype(jnp.bfloat16) for g in range(docs // LANES)], axis=0
    )


def gather_rows(base, ids, tables, count):
    entries = ids.shape[2]
    docs = tables[0].shape[1]
    features = sum(t.shape[0] for t in tables)

    def kernel(base_ref, ids_ref, *refs):
        out_ref = refs[-1]
        hot = one_hot(ids_ref[0], docs)
        start = 0
        for table_ref in refs[:-1]:
            stop = start + table_ref.shape[0]
            out_ref[0, start:stop, :] = dot(table_ref[...], hot).astype(out_ref.dtype)
            start = stop

    return call(
        kernel,
        jax.ShapeDtypeStruct((count, features, entries), tables[0].dtype),
        (count,),
        [pl.BlockSpec((1, 1, entries), lambda b, base: (base[0] + b, 0, 0))]
        + [pl.BlockSpec(t.shape, lambda b, base: (0, 0)) for t in tables],
        pl.BlockSpec((1, features, entries), lambda b, base: (b, 0, 0)),
        1000,
        1000,
        prefetch=1,
    )(base, ids, *tables)


def gather_pieces(me, ids, table, partners):
    entries = ids.shape[2]
    features, docs = table.shape
    count = len(partners)

    def kernel(me_ref, *refs):
        table_ref = refs[count]
        for ids_ref, out_ref in zip(refs[:count], refs[count + 1 :]):
            out_ref[...] = dot(table_ref[...], one_hot(ids_ref[0], docs)).astype(out_ref.dtype)

    return call(
        kernel,
        [jax.ShapeDtypeStruct((features, entries), table.dtype)] * count,
        (1,),
        [pl.BlockSpec((1, 1, entries), lambda i, me, k=k: (me[0] ^ k, 0, 0)) for k in partners]
        + [pl.BlockSpec((features, docs), lambda i, me: (0, 0))],
        [pl.BlockSpec((features, entries), lambda i, me: (0, 0))] * count,
        1000,
        1000,
        prefetch=1,
    )(me, *[ids] * count, table)


def score_near(base, prepared, chosen, width, half):
    queries = prepared.shape[0]
    count, features, entries = chosen.shape
    head = features - width
    stride = width // head

    def kernel(base_ref, own_ref, far_ref, chosen_ref, out_ref):
        part = dot(own_ref[...], chosen_ref[0, :width, :]) + dot(far_ref[...], chosen_ref[0, width:, :])

        @pl.when(pl.program_id(0) == 0)
        def _():
            out_ref[...] = part

        @pl.when(pl.program_id(0) > 0)
        def _():
            out_ref[...] += part

    return call(
        kernel,
        jax.ShapeDtypeStruct((queries, entries), jnp.float32),
        (count,),
        [
            pl.BlockSpec((queries, width), lambda j, base: (0, base[0] + j)),
            pl.BlockSpec((queries, head), lambda j, base: (0, ((base[0] + j) ^ half) * stride)),
            pl.BlockSpec((1, features, entries), lambda j, base: (j, 0, 0)),
        ],
        pl.BlockSpec((queries, entries), lambda j, base: (0, 0)),
        2 * count * features * queries * entries,
        2 * count * features * (queries + entries) + 4 * queries * entries,
        prefetch=1,
    )(base, prepared, prepared, chosen)


def score_pieces(me, prepared, chosen, partners, total, width, scale):
    queries = prepared.shape[0]
    features, entries = chosen[0].shape
    count = len(partners)
    whole = pl.BlockSpec((queries, entries), lambda i, me: (0, 0))

    def kernel(me_ref, *refs):
        out = refs[-2][...]
        for prepared_ref, chosen_ref in zip(refs[:count], refs[count : 2 * count]):
            out = out + dot(prepared_ref[:, width - features :], chosen_ref[...])
        refs[-1][...] = out * scale

    return call(
        kernel,
        jax.ShapeDtypeStruct((queries, entries), jnp.float32),
        (1,),
        [pl.BlockSpec((queries, width), lambda i, me, k=k: (0, me[0] ^ k)) for k in partners]
        + [pl.BlockSpec((features, entries), lambda i, me: (0, 0))] * count
        + [whole],
        whole,
        2 * count * features * queries * entries,
        2 * count * features * (queries + entries) + 8 * queries * entries,
        prefetch=1,
    )(me, *[prepared] * count, *chosen, total)


def score_all(prepared, chosen, scale):
    queries = prepared.shape[0]
    devices, width, entries = chosen.shape

    def kernel(prepared_ref, chosen_ref, out_ref):
        part = dot(prepared_ref[...], chosen_ref[...]) * scale

        @pl.when(pl.program_id(0) == 0)
        def _():
            out_ref[...] = part

        @pl.when(pl.program_id(0) > 0)
        def _():
            out_ref[...] += part

    steps = 4
    block = devices * width // steps
    return call(
        kernel,
        jax.ShapeDtypeStruct((queries, entries), jnp.float32),
        (steps,),
        [
            pl.BlockSpec((queries, block), lambda i: (0, i)),
            pl.BlockSpec((block, entries), lambda i: (i, 0)),
        ],
        pl.BlockSpec((queries, entries), lambda i: (0, 0)),
        2 * devices * width * queries * entries,
        2 * devices * width * (queries + entries) + 4 * queries * entries,
    )(prepared, chosen.reshape(devices * width, entries))


def precondition(queries, left_inv, right_inv):
    total, features = queries.shape
    layers, k_out, _ = left_inv.shape
    k_in = right_inv.shape[1]
    group = MXU // k_out
    pair = MXU // k_in
    left = jnp.einsum("lai,rs->laris", left_inv, jnp.eye(group, dtype=left_inv.dtype)).reshape(
        layers, MXU, MXU
    )
    right = jnp.einsum("rs,ljk->lrjsk", jnp.eye(pair, dtype=right_inv.dtype), right_inv).reshape(
        layers, MXU, MXU
    )
    rows = 64
    wide = k_out // pair
    both = 2 * group

    def kernel(queries_ref, left_ref, right_ref, out_ref, middle_ref):
        for layer in range(layers):
            first = layer * k_out * k_in
            stack = jnp.concatenate(
                [queries_ref[:, first + p * MXU : first + (p + 1) * MXU] for p in range(wide)], axis=0
            )
            middle_ref[...] = dot(stack, right_ref[layer])
            for q in range(0, rows, both):
                halves = []
                for start in (q, q + group):
                    tiles = []
                    for p in range(wide):
                        at = p * rows + start
                        for s in range(pair):
                            tiles.append(middle_ref[at : at + group, s * k_in : (s + 1) * k_in])
                    halves.append(jnp.concatenate(tiles, axis=0))
                middle = jnp.concatenate(halves, axis=1).astype(queries_ref.dtype)
                result = dot(left_ref[layer], middle)
                for a in range(k_out):
                    at = a * group
                    tile = jnp.concatenate(
                        [result[at : at + group, :k_in], result[at : at + group, k_in:]], axis=0
                    )
                    lanes = first + a * k_in
                    out_ref[q : q + both, lanes : lanes + k_in] = tile.astype(out_ref.dtype)

    square = pl.BlockSpec((layers, MXU, MXU), lambda i: (0, 0, 0))
    return call(
        kernel,
        jax.ShapeDtypeStruct(queries.shape, queries.dtype),
        (total // rows,),
        [pl.BlockSpec((rows, features), lambda i: (i, 0)), square, square],
        pl.BlockSpec((rows, features), lambda i: (i, 0)),
        4 * total * features * MXU,
        4 * total * features,
        scratch=[pltpu.VMEM((wide * rows, MXU), jnp.float32)],
    )(queries, left, right)


def on_device(doc_grads, query_grads, left_inv, right_inv, cand_owner, cand_row):
    devices = lax.axis_size("docs")
    half = devices // 2
    me = lax.axis_index("docs").astype(jnp.int32).reshape(1)
    base = me & -half
    doc_count = doc_grads.shape[0] // devices
    entries = cand_row.shape[0]
    width = doc_grads.shape[1]
    scale = query_grads.shape[1] ** (-0.5)

    def swap(values, k):
        return lax.ppermute(values, "docs", [(i, i ^ k) for i in range(devices)])

    head = width // 4 if width % (4 * LANES) == 0 else 0
    if head:
        across = swap(doc_grads[:, :head], half)
    own_ids = cand_owner[:, 0] * doc_count + cand_row
    ids = lax.all_to_all(
        jnp.broadcast_to(own_ids, (devices, 1, entries)), "docs", split_axis=0, concat_axis=0, tiled=True
    )
    table = doc_grads.T
    if not head:
        picked = gather_rows(jnp.zeros((1,), jnp.int32), ids, [table], devices)
        chosen = lax.all_to_all(picked, "docs", split_axis=0, concat_axis=0, tiled=True)
        return score_all(precondition(query_grads, left_inv, right_inv), chosen, scale)

    partners = list(range(half, devices))
    body = table[head:]
    first = gather_pieces(me, ids, body, partners[:2])
    ids, first = lax.optimization_barrier((ids, first))
    rest = gather_pieces(me, ids, body, partners[2:])
    ids, rest = lax.optimization_barrier((ids, rest))
    far = [swap(piece, k) for piece, k in zip([*first, *rest], partners)]
    picked = gather_rows(base, ids, [table, across.T], half)
    query_grads, picked = lax.optimization_barrier((query_grads, picked))
    groups = [list(range(half)), list(range(half, devices))]
    near = lax.all_to_all(
        picked, "docs", split_axis=0, concat_axis=0, axis_index_groups=groups, tiled=True
    )
    prepared = precondition(query_grads, left_inv, right_inv)
    total = score_near(base, prepared, near, width, half)
    last = half - 2
    total = score_pieces(me, prepared, far[:last], partners[:last], total, width, 1.0)
    return score_pieces(me, prepared, far[last:], partners[last:], total, width, scale)


def solution(mesh):
    placed = (
        P("parts", "docs"),
        P(("parts", "docs"), None),
        P(),
        P(),
        P(("parts", "docs"), None),
        P(("parts", "docs")),
    )
    return jax.shard_map(
        on_device, mesh=mesh, in_specs=placed, out_specs=P(("parts", "docs"), None), check_vma=False
    )
```

time: 174 us -> 138 us (0.79)
  the two profiles are of different devices: /device:TPU:15 before, /device:TPU:0 now
where the time goes in v3:
time: 138 us
  waiting for transfers between devices  51.1 us (37%)
  Pallas kernels  35.4 us (26%)
  starting transfers between devices  30.2 us (22%)
  local copies, waits for them, and re-layouts  18.2 us (13%)
  other arithmetic  2.58 us (2%)
    ppermute x9, waiting for transfers between devices, swap(): return lax.ppermute(values, 'docs', [(i, i ^ k) for i in range(devices)])  32.5 us
    ppermute x9, starting transfers between devices, swap(): return lax.ppermute(values, 'docs', [(i, i ^ k) for i in range(devices)])  22.6 us
    all_to_all x1, waiting for transfers between devices, on_device(): lax.all_to_all(jnp.broadcast_to(own_ids, (devices, 1, entries)), 'docs',...  18.6 us
    pallas_call x1, Pallas kernels, precondition(): call(kernel, jax.ShapeDtypeStruct(queries.shape, queries.dtype), (total /...  12.7 us
    unnamed x23, local copies, waits for them, and re-layouts  9.27 us
    pallas_call x1, Pallas kernels, gather_rows(): call(kernel, jax.ShapeDtypeStruct((count, features, entries), tables[0].d...  6.96 us
    reshape x1, local copies, waits for them, and re-layouts, precondition(): jnp.einsum('lai,rs->laris', left_inv, jnp.eye(group, dtype=left_inv.dtype))  6.89 us
    pallas_call x1, Pallas kernels, score_near(): call(kernel, jax.ShapeDtypeStruct((queries, entries), jnp.float32), (coun...  6.46 us
  transfers between devices with their start and end apart: 11, of which 6 were waited for; matrix products, arithmetic and copies ran while one was open for 8% of the time, Pallas kernels for 19%

profile of v3, /device:TPU:0, one launch (start us, length us, event | category | flops | bytes accessed | tf_op | source)
XLA Modules:
  0.0 137.7 jit_solution(5731490674229265810)
XLA Ops:
  0.0 0.0 copy-start.10
  0.0 0.0 copy-start.9
  0.0 3.0 %copy.9 = bf16[2048,512]{0,1:T(8,128)(2,1)S(1)} copy(bf16[2048,512]{1,0:T(8,128)(2,1)} %param.6) | data formatting | bytes 4194304 | tf_op args[0]
  3.0 4.1 %collective-permute-start = (bf16[2048,128]{0,1:T(8,128)(2,1)S(1)}, bf16[2048,128]{0,1:T(8,128)(2,1)S(1)}, u32[]{:S(2)}, u32[]{:S(2)}) collective-permute-start(bf16[2048,128]{0,1:T(8,128)(2,1)S(1)} %slice.9), channel_id=1, source_target_pairs={{0,8},{1,9},{2,10},{3,11},{4,12},{5,13},{6,14},{7,15},{8,0},{9,1},... | collective-permute-start | bytes 1572872 | tf_op jit(solution)/shard_map/ppermute | solution.py:248
  7.1 0.0 copy-done.10
  7.1 0.0 copy-done.9
  7.1 0.6 broadcast_in_dim.3
  7.7 3.9 %all-to-all-start = ((s32[16,1,256]{2,1,0:T(1,128)}), s32[16,1,256]{2,1,0:T(1,128)S(1)}, u32[]{:S(2)}, u32[]{:S(2)}) async-start(s32[16,1,256]{2,1,0:T(1,128)} %broadcast_in_dim.3), calls=%async_computation | async-start | bytes 32768 | tf_op jit(solution)/shard_map/all_to_all | solution.py:254
  11.7 1.3 slice.8.refs_2_.refs_6_
  12.9 18.6 %all-to-all-done.refs_0_.refs_1_.refs_2_.refs_3_.refs_4_.refs_5_.ids_ref = s32[16,1,256]{2,1,0:T(1,128)S(1)} async-done(((s32[16,1,256]{2,1,0:T(1,128)}), s32[16,1,256]{2,1,0:T(1,128)S(1)}, u32[]{:S(2)}, u32[]{:S(2)}) %all-to-all-start) | async-done | bytes 16416 | tf_op jit(solution)/shard_map/all_to_all | solution.py:254
  31.5 0.0 copy-start
  31.5 1.4 %copy-done = bf16[384,2048]{1,0:T(8,128)(2,1)S(1)} copy-done((bf16[384,2048]{1,0:T(8,128)(2,1)S(1)}, bf16[384,2048]{1,0:T(8,128)(2,1)}, u32[]{:S(2)}) %copy-start) | copy-done | bytes 1572888
  33.0 1.0 shard_map.64
  34.0 0.0 copy-start.4
  34.0 0.7 copy-done.4
  34.6 0.0 copy-start.5
  34.6 0.7 copy-done.5
  35.3 2.6 %shard_map.65 = (bf16[384,256]{1,0:T(8,128)(2,1)}, bf16[384,256]{1,0:T(8,128)(2,1)}, bf16[384,256]{1,0:T(8,128)(2,1)}, bf16[384,256]{1,0:T(8,128)(2,1)S(1)}, bf1...) custom-call(s32[1]{0:T(128)} %bitcast.me_ref, ...), custom_call_target="tpu_custom_call" | custom-call | flops 1000 | bytes 1000 | tf_op jit(solution)/shard_map/pallas_call | solution.py:79
  37.9 0.0 copy-start.2
  37.9 0.7 copy-done.2
  38.6 0.0 copy-start.3
  38.6 0.7 copy-done.3
  39.3 0.0 copy-start.6
  39.3 0.7 copy-done.6
  39.9 0.0 collective-permute-done
  39.9 0.0 copy-start.7
  40.0 7.0 %shard_map.66 = bf16[8,640,256]{2,1,0:T(8,128)(2,1)S(1)} custom-call(s32[1]{0:T(128)S(6)} %and.4.base_ref, s32[16,1,256]{2,1,0:T(1,128)S(1)} %all-to-all-done.refs_0_.refs_1_.refs_2_.refs_3_.refs_4_.refs_5_.ids_ref, bf16[512,2048]{1,0:T(8,128)(2,1)S(1)} %bitcast.11, bf16[128,2048]{1,0:T(8,128)(2,1)S(1)} %bitcast.12), custom_call_target="tpu_custom_call" | custom-call | flops 1000 | bytes 1000 | tf_op jit(solution)/shard_map/pallas_call | solution.py:56
  46.9 0.0 copy-start.1
  46.9 1.6 %copy-done.1 = bf16[8,640,256]{2,1,0:T(8,128)(2,1)} copy-done((bf16[8,640,256]{2,1,0:T(8,128)(2,1)}, bf16[8,640,256]{2,1,0:T(8,128)(2,1)S(1)}, u32[]{:S(2)}) %copy-start.1) | copy-done | bytes 2621464
  48.5 0.0 copy-start.8
  48.5 3.8 %all-to-all-start.1 = ((bf16[8,640,256]{2,1,0:T(8,128)(2,1)}), bf16[8,640,256]{2,1,0:T(8,128)(2,1)S(1)}, u32[]{:S(2)}, u32[]{:S(2)}) async-start(bf16[8,640,256]{2,1,0:T(8,128)(2,1)} %copy-done.1), calls=%async_computation.1 | async-start | bytes 5242880 | tf_op jit(solution)/shard_map/all_to_all | solution.py:273
  52.3 0.0 copy-done.7
  52.3 0.3 multiply_bitcast_fusion.1
  52.6 0.2 reshape.13.right_ref
  52.7 4.1 %collective-permute-start.5 = (bf16[384,256]{1,0:T(8,128)(2,1)}, bf16[384,256]{1,0:T(8,128)(2,1)S(1)}, u32[]{:S(2)}, u32[]{:S(2)}) collective-permute-start(bf16[384,256]{1,0:T(8,128)(2,1)} %get-tuple-element.40), channel_id=1, source_target_pairs={{0,10},{1,11},{2,8},{3,9},{4,14},{5,15},{6,12},{7,13},{8,2},{9,3},... | collective-permute-start | bytes 589832 | tf_op jit(solution)/shard_map/ppermute | solution.py:248
  56.8 0.0 collective-permute-start.6
  56.8 3.3 %collective-permute-start.7 = (bf16[384,256]{1,0:T(8,128)(2,1)}, bf16[384,256]{1,0:T(8,128)(2,1)}, u32[]{:S(2)}, u32[]{:S(2)}) collective-permute-start(bf16[384,256]{1,0:T(8,128)(2,1)} %get-tuple-element.42), channel_id=1, source_target_pairs={{0,12},{1,13},{2,14},{3,15},{4,8},{5,9},{6,10},{7,11},{8,4},{9,5},... | collective-permute-start | bytes 589832 | tf_op jit(solution)/shard_map/ppermute | solution.py:248
  60.2 0.0 copy-done.8
  60.2 2.3 %multiply_bitcast_fusion = bf16[2,32,8,32,8]{4,3,2,1,0:T(8,128)(2,1)} fusion(bf16[2,32,32]{2,1,0:T(8,128)(2,1)S(1)} %copy-done.8, bf16[8,8]{1,0:T(8,128)(2,1)S(1)} %fusion), kind=kLoop, calls=%fused_computation | loop fusion | flops 131072 | bytes 266368 | tf_op jit(solution)/shard_map/lai,rs->laris/transpose | solution.py:188
  62.4 6.9 %reshape.12.left_ref = bf16[2,256,256]{2,1,0:T(8,128)(2,1)S(1)} reshape(bf16[2,32,8,32,8]{4,3,2,1,0:T(8,128)(2,1)} %multiply_bitcast_fusion) | data formatting | bytes 524288 | tf_op jit(solution)/shard_map/reshape | solution.py:188
  69.3 1.2 collective-permute-start.1
  70.5 3.3 %collective-permute-start.2 = (bf16[384,256]{1,0:T(8,128)(2,1)}, bf16[384,256]{1,0:T(8,128)(2,1)}, u32[]{:S(2)}, u32[]{:S(2)}) collective-permute-start(bf16[384,256]{1,0:T(8,128)(2,1)} %copy-done.2), channel_id=1, source_target_pairs={{0,15},{1,14},{2,13},{3,12},{4,11},{5,10},{6,9},{7,8},{8,7},{9,6},... | collective-permute-start | bytes 589832 | tf_op jit(solution)/shard_map/ppermute | solution.py:248
  73.8 12.1 %collective-permute-done.5.refs_8_ = bf16[384,256]{1,0:T(8,128)(2,1)S(1)} collective-permute-done((bf16[384,256]{1,0:T(8,128)(2,1)}, bf16[384,256]{1,0:T(8,128)(2,1)S(1)}, u32[]{:S(2)}, u32[]{:S(2)}) %collective-permute-start.5) | collective-permute-done | bytes 196640 | tf_op jit(solution)/shard_map/ppermute | solution.py:248
  85.9 2.8 %collective-permute-start.8 = (bf16[384,256]{1,0:T(8,128)(2,1)}, bf16[384,256]{1,0:T(8,128)(2,1)}, u32[]{:S(2)}, u32[]{:S(2)}) collective-permute-start(bf16[384,256]{1,0:T(8,128)(2,1)} %copy-done.6), channel_id=1, source_target_pairs={{0,13},{1,12},{2,15},{3,14},{4,9},{5,8},{6,11},{7,10},{8,5},{9,4},... | collective-permute-start | bytes 589832 | tf_op jit(solution)/shard_map/ppermute | solution.py:248
  88.7 1.4 %collective-permute-done.6.refs_9_ = bf16[384,256]{1,0:T(8,128)(2,1)} collective-permute-done((bf16[384,256]{1,0:T(8,128)(2,1)}, bf16[384,256]{1,0:T(8,128)(2,1)}, u32[]{:S(2)}, u32[]{:S(2)}) %collective-permute-start.6) | collective-permute-done | bytes 196640 | tf_op jit(solution)/shard_map/ppermute | solution.py:248
  90.2 3.8 %collective-permute-start.3 = (bf16[384,256]{1,0:T(8,128)(2,1)}, bf16[384,256]{1,0:T(8,128)(2,1)}, u32[]{:S(2)}, u32[]{:S(2)}) collective-permute-start(bf16[384,256]{1,0:T(8,128)(2,1)} %copy-done.5), channel_id=1, source_target_pairs={{0,8},{1,9},{2,10},{3,11},{4,12},{5,13},{6,14},{7,15},{8,0},{9,1},... | collective-permute-start | bytes 589832 | tf_op jit(solution)/shard_map/ppermute | solution.py:248
  94.0 5.0 %collective-permute-done.7.refs_10_ = bf16[384,256]{1,0:T(8,128)(2,1)} collective-permute-done((bf16[384,256]{1,0:T(8,128)(2,1)}, bf16[384,256]{1,0:T(8,128)(2,1)}, u32[]{:S(2)}, u32[]{:S(2)}) %collective-permute-start.7) | collective-permute-done | bytes 196640 | tf_op jit(solution)/shard_map/ppermute | solution.py:248
  99.0 0.0 collective-permute-start.4
  99.0 12.7 %shard_map.67.own_ref.far_ref.refs_0_.refs_1_.refs_2_.refs_3_.refs_4_.refs_5_ = bf16[512,8192]{1,0:T(8,128)(2,1)} custom-call(bf16[512,8192]{1,0:T(8,128)(2,1)} %queries_ref, bf16[2,256,256]{2,1,0:T(8,128)(2,1)S(1)} %reshape.12.left_ref, bf16[2,256,256]{2,1,0:T(8,128)(2,1)S(1)} %reshape.13.right_ref), custom_call_target="tpu_custom_call" | custom-call | flops 4294967296 | bytes 16777216 | tf_op jit(solution)/shard_map/pallas_call | solution.py:225
  111.7 0.0 all-to-all-done.1.chosen_ref
  111.7 6.5 %shard_map.68.refs_12_ = f32[512,256]{1,0:T(8,128)S(1)} custom-call(s32[1]{0:T(128)S(6)} %and.4.base_ref, bf16[512,8192]{1,0:T(8,128)(2,1)} %shard_map.67.own_ref.far_ref.refs_0_.refs_1_.refs_2_.refs_3_.refs_4_.refs_5_, bf16[512,8192]{1,0:T(8,128)(2,1)} %shard_map.67.own_ref.far_ref.refs_0_.refs_1_.refs_2_.refs_3_.refs_4_.refs_5_, ...), custom_call_target="tpu_custom_call" | custom-call | flops 1342177280 | bytes 8388608 | tf_op jit(solution)/shard_map/pallas_call | solution.py:109
  118.2 0.0 collective-permute-done.8.refs_11_
  118.2 9.6 %collective-permute-done.3.refs_6_ = bf16[384,256]{1,0:T(8,128)(2,1)} collective-permute-done((bf16[384,256]{1,0:T(8,128)(2,1)}, bf16[384,256]{1,0:T(8,128)(2,1)}, u32[]{:S(2)}, u32[]{:S(2)}) %collective-permute-start.3) | collective-permute-done | bytes 196640 | tf_op jit(solution)/shard_map/ppermute | solution.py:248
  127.8 4.3 %collective-permute-done.4.refs_7_ = bf16[384,256]{1,0:T(8,128)(2,1)} collective-permute-done((bf16[384,256]{1,0:T(8,128)(2,1)}, bf16[384,256]{1,0:T(8,128)(2,1)}, u32[]{:S(2)}, u32[]{:S(2)}) %collective-permute-start.4) | collective-permute-done | bytes 196640 | tf_op jit(solution)/shard_map/ppermute | solution.py:248
  132.1 3.1 %shard_map.69.refs_4_ = f32[512,256]{1,0:T(8,128)S(1)} custom-call(s32[1]{0:T(128)} %bitcast.me_ref, bf16[512,8192]{1,0:T(8,128)(2,1)} %shard_map.67.own_ref.far_ref.refs_0_.refs_1_.refs_2_.refs_3_.refs_4_.refs_5_, bf16[512,8192]{1,0:T(8,128)(2,1)} %shard_map.67.own_ref.far_ref.refs_0_.refs_1_.refs_2_.refs_3_.refs_4_.refs_5_, ...), custom_call_target="tpu_custom_call" | custom-call | flops 603979776 | bytes 4587520 | tf_op jit(solution)/shard_map/pallas_call | solution.py:137
  135.2 0.0 collective-permute-done.1.refs_2_
  135.2 0.0 collective-permute-done.2.refs_3_
  135.2 2.5 %shard_map.70 = f32[512,256]{1,0:T(8,128)} custom-call(s32[1]{0:T(128)} %bitcast.me_ref, bf16[512,8192]{1,0:T(8,128)(2,1)} %shard_map.67.own_ref.far_ref.refs_0_.refs_1_.refs_2_.refs_3_.refs_4_.refs_5_, bf16[512,8192]{1,0:T(8,128)(2,1)} %shard_map.67.own_ref.far_ref.refs_0_.refs_1_.refs_2_.refs_3_.refs_4_.refs_5_, ...), custom_call_target="tpu_custom_call" | custom-call | flops 201326592 | bytes 2228224 | tf_op jit(solution)/shard_map/pallas_call | solution.py:137
  (5 shorter events, 0.1 us)
Async XLA Ops:
  0.0 7.1 %copy-start.10 = (s32[256,1]{0,1:T(1,128)S(1)}, s32[256,1]{0,1:T(1,128)}, u32[]{:S(2)}) copy-start(s32[256,1]{0,1:T(1,128)} %param.10) | copy-start | bytes 3076
  0.0 7.1 %copy-start.9 = (s32[256]{0:T(256)S(1)}, s32[256]{0:T(256)}, u32[]{:S(2)}) copy-start(s32[256]{0:T(256)} %param.11) | copy-start | bytes 3076
  3.0 36.9 %collective-permute-start = (bf16[2048,128]{0,1:T(8,128)(2,1)S(1)}, bf16[2048,128]{0,1:T(8,128)(2,1)S(1)}, u32[]{:S(2)}, u32[]{:S(2)}) collective-permute-start(bf16[2048,128]{0,1:T(8,128)(2,1)S(1)} %slice.9), channel_id=1, source_target_pairs={{0,8},{1,9},{2,10},{3,11},{4,12},{5,13},{6,14},{7,15},{8,0},{9,1},... | collective-permute-start | bytes 1572872 | tf_op jit(solution)/shard_map/ppermute | solution.py:248
  7.7 23.8 %all-to-all-start = ((s32[16,1,256]{2,1,0:T(1,128)}), s32[16,1,256]{2,1,0:T(1,128)S(1)}, u32[]{:S(2)}, u32[]{:S(2)}) async-start(s32[16,1,256]{2,1,0:T(1,128)} %broadcast_in_dim.3), calls=%async_computation | async-start | bytes 32768 | tf_op jit(solution)/shard_map/all_to_all | solution.py:254
  31.5 1.4 %copy-start = (bf16[384,2048]{1,0:T(8,128)(2,1)S(1)}, bf16[384,2048]{1,0:T(8,128)(2,1)}, u32[]{:S(2)}) copy-start(bf16[384,2048]{1,0:T(8,128)(2,1)} %slice.8.refs_2_.refs_6_) | copy-start | bytes 4718596
  34.0 0.7 copy-start.4
  34.6 0.7 copy-start.5
  37.9 0.7 copy-start.2
  38.6 0.7 copy-start.3
  39.3 0.7 copy-start.6
  39.9 12.3 %copy-start.7 = (bf16[2,128,128]{2,1,0:T(8,128)(2,1)S(1)}, bf16[2,128,128]{2,1,0:T(8,128)(2,1)}, u32[]{:S(2)}) copy-start(bf16[2,128,128]{2,1,0:T(8,128)(2,1)} %param.9) | copy-start | bytes 196612
  46.9 1.6 %copy-start.1 = (bf16[8,640,256]{2,1,0:T(8,128)(2,1)}, bf16[8,640,256]{2,1,0:T(8,128)(2,1)S(1)}, u32[]{:S(2)}) copy-start(bf16[8,640,256]{2,1,0:T(8,128)(2,1)S(1)} %shard_map.66) | copy-start | bytes 7864324
  48.5 11.7 %copy-start.8 = (bf16[2,32,32]{2,1,0:T(8,128)(2,1)S(1)}, bf16[2,32,32]{2,1,0:T(8,128)(2,1)}, u32[]{:S(2)}) copy-start(bf16[2,32,32]{2,1,0:T(8,128)(2,1)} %param.8) | copy-start | bytes 12292
  48.5 63.2 %all-to-all-start.1 = ((bf16[8,640,256]{2,1,0:T(8,128)(2,1)}), bf16[8,640,256]{2,1,0:T(8,128)(2,1)S(1)}, u32[]{:S(2)}, u32[]{:S(2)}) async-start(bf16[8,640,256]{2,1,0:T(8,128)(2,1)} %copy-done.1), calls=%async_computation.1 | async-start | bytes 5242880 | tf_op jit(solution)/shard_map/all_to_all | solution.py:273
  52.7 33.2 %collective-permute-start.5 = (bf16[384,256]{1,0:T(8,128)(2,1)}, bf16[384,256]{1,0:T(8,128)(2,1)S(1)}, u32[]{:S(2)}, u32[]{:S(2)}) collective-permute-start(bf16[384,256]{1,0:T(8,128)(2,1)} %get-tuple-element.40), channel_id=1, source_target_pairs={{0,10},{1,11},{2,8},{3,9},{4,14},{5,15},{6,12},{7,13},{8,2},{9,3},... | collective-permute-start | bytes 589832 | tf_op jit(solution)/shard_map/ppermute | solution.py:248
  56.8 33.3 %collective-permute-start.6 = (bf16[384,256]{1,0:T(8,128)(2,1)}, bf16[384,256]{1,0:T(8,128)(2,1)}, u32[]{:S(2)}, u32[]{:S(2)}) collective-permute-start(bf16[384,256]{1,0:T(8,128)(2,1)} %get-tuple-element.41), channel_id=1, source_target_pairs={{0,11},{1,10},{2,9},{3,8},{4,15},{5,14},{6,13},{7,12},{8,3},{9,2},... | collective-permute-start | bytes 589832 | tf_op jit(solution)/shard_map/ppermute | solution.py:248
  56.8 42.1 %collective-permute-start.7 = (bf16[384,256]{1,0:T(8,128)(2,1)}, bf16[384,256]{1,0:T(8,128)(2,1)}, u32[]{:S(2)}, u32[]{:S(2)}) collective-permute-start(bf16[384,256]{1,0:T(8,128)(2,1)} %get-tuple-element.42), channel_id=1, source_target_pairs={{0,12},{1,13},{2,14},{3,15},{4,8},{5,9},{6,10},{7,11},{8,4},{9,5},... | collective-permute-start | bytes 589832 | tf_op jit(solution)/shard_map/ppermute | solution.py:248
  69.3 65.9 %collective-permute-start.1 = (bf16[384,256]{1,0:T(8,128)(2,1)}, bf16[384,256]{1,0:T(8,128)(2,1)S(1)}, u32[]{:S(2)}, u32[]{:S(2)}) collective-permute-start(bf16[384,256]{1,0:T(8,128)(2,1)} %copy-done.3), channel_id=1, source_target_pairs={{0,14},{1,15},{2,12},{3,13},{4,10},{5,11},{6,8},{7,9},{8,6},{9,7},... | collective-permute-start | bytes 589832 | tf_op jit(solution)/shard_map/ppermute | solution.py:248
  70.5 64.7 %collective-permute-start.2 = (bf16[384,256]{1,0:T(8,128)(2,1)}, bf16[384,256]{1,0:T(8,128)(2,1)}, u32[]{:S(2)}, u32[]{:S(2)}) collective-permute-start(bf16[384,256]{1,0:T(8,128)(2,1)} %copy-done.2), channel_id=1, source_target_pairs={{0,15},{1,14},{2,13},{3,12},{4,11},{5,10},{6,9},{7,8},{8,7},{9,6},... | collective-permute-start | bytes 589832 | tf_op jit(solution)/shard_map/ppermute | solution.py:248
  85.9 32.2 %collective-permute-start.8 = (bf16[384,256]{1,0:T(8,128)(2,1)}, bf16[384,256]{1,0:T(8,128)(2,1)}, u32[]{:S(2)}, u32[]{:S(2)}) collective-permute-start(bf16[384,256]{1,0:T(8,128)(2,1)} %copy-done.6), channel_id=1, source_target_pairs={{0,13},{1,12},{2,15},{3,14},{4,9},{5,8},{6,11},{7,10},{8,5},{9,4},... | collective-permute-start | bytes 589832 | tf_op jit(solution)/shard_map/ppermute | solution.py:248
  90.2 37.7 %collective-permute-start.3 = (bf16[384,256]{1,0:T(8,128)(2,1)}, bf16[384,256]{1,0:T(8,128)(2,1)}, u32[]{:S(2)}, u32[]{:S(2)}) collective-permute-start(bf16[384,256]{1,0:T(8,128)(2,1)} %copy-done.5), channel_id=1, source_target_pairs={{0,8},{1,9},{2,10},{3,11},{4,12},{5,13},{6,14},{7,15},{8,0},{9,1},... | collective-permute-start | bytes 589832 | tf_op jit(solution)/shard_map/ppermute | solution.py:248
  99.0 33.1 %collective-permute-start.4 = (bf16[384,256]{1,0:T(8,128)(2,1)}, bf16[384,256]{1,0:T(8,128)(2,1)}, u32[]{:S(2)}, u32[]{:S(2)}) collective-permute-start(bf16[384,256]{1,0:T(8,128)(2,1)} %copy-done.4), channel_id=1, source_target_pairs={{0,9},{1,8},{2,11},{3,10},{4,13},{5,12},{6,15},{7,14},{8,1},{9,0},... | collective-permute-start | bytes 589832 | tf_op jit(solution)/shard_map/ppermute | solution.py:248

commit v4 on v3

--- a/solution.py
+++ b/solution.py
@@ -55,7 +55,7 @@
 
     return call(
         kernel,
-        jax.ShapeDtypeStruct((count, features, entries), tables[0].dtype),
+        pltpu.HBM((count, features, entries), tables[0].dtype),
         (count,),
         [pl.BlockSpec((1, 1, entries), lambda b, base: (base[0] + b, 0, 0))]
         + [pl.BlockSpec(t.shape, lambda b, base: (0, 0)) for t in tables],
@@ -78,7 +78,7 @@
 
     return call(
         kernel,
-        [jax.ShapeDtypeStruct((features, entries), table.dtype)] * count,
+        [pltpu.HBM((features, entries), table.dtype)] * count,
         (1,),
         [pl.BlockSpec((1, 1, entries), lambda i, me, k=k: (me[0] ^ k, 0, 0)) for k in partners]
         + [pl.BlockSpec((features, docs), lambda i, me: (0, 0))],
@@ -89,14 +89,12 @@
     )(me, *[ids] * count, table)
 
 
-def score_near(base, prepared, chosen, width, half):
+def score_near(base, prepared, chosen):
     queries = prepared.shape[0]
-    count, features, entries = chosen.shape
-    head = features - width
-    stride = width // head
-
-    def kernel(base_ref, own_ref, far_ref, chosen_ref, out_ref):
-        part = dot(own_ref[...], chosen_ref[0, :width, :]) + dot(far_ref[...], chosen_ref[0, width:, :])
+    count, width, entries = chosen.shape
+
+    def kernel(base_ref, prepared_ref, chosen_ref, out_ref):
+        part = dot(prepared_ref[...], chosen_ref[0])
 
         @pl.when(pl.program_id(0) == 0)
         def _():
@@ -112,26 +110,25 @@
         (count,),
         [
             pl.BlockSpec((queries, width), lambda j, base: (0, base[0] + j)),
-            pl.BlockSpec((queries, head), lambda j, base: (0, ((base[0] + j) ^ half) * stride)),
-            pl.BlockSpec((1, features, entries), lambda j, base: (j, 0, 0)),
+            pl.BlockSpec((1, width, entries), lambda j, base: (j, 0, 0)),
         ],
         pl.BlockSpec((queries, entries), lambda j, base: (0, 0)),
-        2 * count * features * queries * entries,
-        2 * count * features * (queries + entries) + 4 * queries * entries,
+        2 * count * width * queries * entries,
+        2 * count * width * (queries + entries) + 4 * queries * entries,
         prefetch=1,
-    )(base, prepared, prepared, chosen)
-
-
-def score_pieces(me, prepared, chosen, partners, total, width, scale):
+    )(base, prepared, chosen)
+
+
+def score_pieces(me, prepared, chosen, partners, total, scale):
     queries = prepared.shape[0]
-    features, entries = chosen[0].shape
+    width, entries = chosen[0].shape
     count = len(partners)
     whole = pl.BlockSpec((queries, entries), lambda i, me: (0, 0))
 
     def kernel(me_ref, *refs):
         out = refs[-2][...]
         for prepared_ref, chosen_ref in zip(refs[:count], refs[count : 2 * count]):
-            out = out + dot(prepared_ref[:, width - features :], chosen_ref[...])
+            out = out + dot(prepared_ref[...], chosen_ref[...])
         refs[-1][...] = out * scale
 
     return call(
@@ -139,11 +136,11 @@
         jax.ShapeDtypeStruct((queries, entries), jnp.float32),
         (1,),
         [pl.BlockSpec((queries, width), lambda i, me, k=k: (0, me[0] ^ k)) for k in partners]
-        + [pl.BlockSpec((features, entries), lambda i, me: (0, 0))] * count
+        + [pl.BlockSpec((width, entries), lambda i, me: (0, 0))] * count
         + [whole],
         whole,
-        2 * count * features * queries * entries,
-        2 * count * features * (queries + entries) + 8 * queries * entries,
+        2 * count * width * queries * entries,
+        2 * count * width * (queries + entries) + 8 * queries * entries,
         prefetch=1,
     )(me, *[prepared] * count, *chosen, total)
 
@@ -185,17 +182,39 @@
     k_in = right_inv.shape[1]
     group = MXU // k_out
     pair = MXU // k_in
-    left = jnp.einsum("lai,rs->laris", left_inv, jnp.eye(group, dtype=left_inv.dtype)).reshape(
-        layers, MXU, MXU
-    )
-    right = jnp.einsum("rs,ljk->lrjsk", jnp.eye(pair, dtype=right_inv.dtype), right_inv).reshape(
-        layers, MXU, MXU
-    )
     rows = 64
     wide = k_out // pair
     both = 2 * group
 
-    def kernel(queries_ref, left_ref, right_ref, out_ref, middle_ref):
+    def spread(values, times):
+        size = values.shape[0]
+        rows = lax.broadcasted_iota(jnp.int32, (MXU, size), 0) // times
+        picks = (rows == lax.broadcasted_iota(jnp.int32, (MXU, size), 1)).astype(values.dtype)
+        wide = dot(picks, values).astype(values.dtype)
+        wide = lax.dot_general(
+            wide, picks, (((1,), (1,)), ((), ())), preferred_element_type=jnp.float32
+        )
+        row = lax.broadcasted_iota(jnp.int32, (MXU, MXU), 0) % times
+        column = lax.broadcasted_iota(jnp.int32, (MXU, MXU), 1) % times
+        return jnp.where(row == column, wide, 0.0).astype(values.dtype)
+
+    def repeat(values, times):
+        empty = jnp.zeros_like(values)
+        return jnp.concatenate(
+            [
+                jnp.concatenate([values if i == j else empty for j in range(times)], axis=1)
+                for i in range(times)
+            ],
+            axis=0,
+        )
+
+    def kernel(queries_ref, left_inv_ref, right_inv_ref, out_ref, middle_ref, left_ref, right_ref):
+        @pl.when(pl.program_id(0) == 0)
+        def _():
+            for layer in range(layers):
+                left_ref[layer] = spread(left_inv_ref[layer], group)
+                right_ref[layer] = repeat(right_inv_ref[layer], pair)
+
         for layer in range(layers):
             first = layer * k_out * k_in
             stack = jnp.concatenate(
@@ -221,17 +240,28 @@
                     lanes = first + a * k_in
                     out_ref[q : q + both, lanes : lanes + k_in] = tile.astype(out_ref.dtype)
 
-    square = pl.BlockSpec((layers, MXU, MXU), lambda i: (0, 0, 0))
     return call(
         kernel,
         jax.ShapeDtypeStruct(queries.shape, queries.dtype),
         (total // rows,),
-        [pl.BlockSpec((rows, features), lambda i: (i, 0)), square, square],
+        [
+            pl.BlockSpec((rows, features), lambda i: (i, 0)),
+            pl.BlockSpec(left_inv.shape, lambda i: (0, 0, 0)),
+            pl.BlockSpec(right_inv.shape, lambda i: (0, 0, 0)),
+        ],
         pl.BlockSpec((rows, features), lambda i: (i, 0)),
         4 * total * features * MXU,
         4 * total * features,
-        scratch=[pltpu.VMEM((wide * rows, MXU), jnp.float32)],
-    )(queries, left, right)
+        scratch=[
+            pltpu.VMEM((wide * rows, MXU), jnp.float32),
+            pltpu.VMEM((layers, MXU, MXU), left_inv.dtype),
+            pltpu.VMEM((layers, MXU, MXU), right_inv.dtype),
+        ],
+    )(queries, left_inv, right_inv)
+
+
+def after(value, *earlier):
+    return lax.optimization_barrier((value, *earlier))[0]
 
 
 def on_device(doc_grads, query_grads, left_inv, right_inv, cand_owner, cand_row):
@@ -247,37 +277,41 @@
     def swap(values, k):
         return lax.ppermute(values, "docs", [(i, i ^ k) for i in range(devices)])
 
-    head = width // 4 if width % (4 * LANES) == 0 else 0
-    if head:
-        across = swap(doc_grads[:, :head], half)
     own_ids = cand_owner[:, 0] * doc_count + cand_row
     ids = lax.all_to_all(
         jnp.broadcast_to(own_ids, (devices, 1, entries)), "docs", split_axis=0, concat_axis=0, tiled=True
     )
     table = doc_grads.T
-    if not head:
+    if width % (4 * LANES):
         picked = gather_rows(jnp.zeros((1,), jnp.int32), ids, [table], devices)
         chosen = lax.all_to_all(picked, "docs", split_axis=0, concat_axis=0, tiled=True)
         return score_all(precondition(query_grads, left_inv, right_inv), chosen, scale)
 
     partners = list(range(half, devices))
-    body = table[head:]
-    first = gather_pieces(me, ids, body, partners[:2])
-    ids, first = lax.optimization_barrier((ids, first))
-    rest = gather_pieces(me, ids, body, partners[2:])
-    ids, rest = lax.optimization_barrier((ids, rest))
-    far = [swap(piece, k) for piece, k in zip([*first, *rest], partners)]
-    picked = gather_rows(base, ids, [table, across.T], half)
-    query_grads, picked = lax.optimization_barrier((query_grads, picked))
-    groups = [list(range(half)), list(range(half, devices))]
+    far = [
+        swap(piece, k)
+        for piece, k in zip(gather_pieces(me, ids, table, partners[:2]), partners[:2])
+    ]
+    ids = after(ids, far[0])
+    far += [
+        swap(piece, k)
+        for piece, k in zip(gather_pieces(me, ids, table, partners[2:]), partners[2:])
+    ]
+    ids = after(ids, far[1])
+    picked = gather_rows(base, ids, [table], half)
     near = lax.all_to_all(
-        picked, "docs", split_axis=0, concat_axis=0, axis_index_groups=groups, tiled=True
-    )
-    prepared = precondition(query_grads, left_inv, right_inv)
-    total = score_near(base, prepared, near, width, half)
-    last = half - 2
-    total = score_pieces(me, prepared, far[:last], partners[:last], total, width, 1.0)
-    return score_pieces(me, prepared, far[last:], partners[last:], total, width, scale)
+        picked,
+        "docs",
+        split_axis=0,
+        concat_axis=0,
+        axis_index_groups=[list(range(half)), list(range(half, devices))],
+        tiled=True,
+    )
+    prepared = precondition(after(query_grads, picked, far[2]), left_inv, right_inv)
+    total = score_near(base, prepared, near)
+    middle = half // 2
+    total = score_pieces(me, prepared, far[:middle], partners[:middle], total, 1.0)
+    return score_pieces(me, prepared, far[middle:], partners[middle:], total, scale)
 
 
 def solution(mesh):

time: 138 us -> 137 us (level)
  waiting for transfers between devices: 51.1 us -> 66.7 us
  local copies, waits for them, and re-layouts: 18.2 us -> 3.56 us
  starting transfers between devices: 30.2 us -> 26.5 us
  Pallas kernels: 35.4 us -> 37.5 us
    ppermute x9 -> x8, waiting for transfers between devices: 32.5 us -> 55.5 us  [swap(): return lax.ppermute(values, 'docs', [(i, i ^ k) for i in range(devices)])]
    all_to_all x1, waiting for transfers between devices: 18.6 us -> 3.55 us  [on_device(): lax.all_to_all(jnp.broadcast_to(own_ids, (devices, 1, entries)), 'docs',...]
    ppermute x9 -> x8, starting transfers between devices: 22.6 us -> 14.8 us  [swap(): return lax.ppermute(values, 'docs', [(i, i ^ k) for i in range(devices)])]
    all_to_all x1, waiting for transfers between devices: 0.01 us -> 7.73 us  [on_device(): lax.all_to_all(picked, 'docs', split_axis=0, concat_axis=0, axis_index_gr...]
    reshape x2 -> x0, local copies, waits for them, and re-layouts: 7.06 us -> none  [the longest x1 6.89 us: precondition(): jnp.einsum('lai,rs->laris', left_inv, jnp.eye(group, dtype=left_inv.dtype))]
    unnamed x23 -> x5, local copies, waits for them, and re-layouts: 9.27 us -> 2.95 us
    all_to_all x1, starting transfers between devices: 3.91 us -> 7.39 us  [on_device(): lax.all_to_all(jnp.broadcast_to(own_ids, (devices, 1, entries)), 'docs',...]
    transpose x2 -> x0, other arithmetic: 2.56 us -> none  [the longest x1 2.28 us: precondition(): jnp.einsum('lai,rs->laris', left_inv, jnp.eye(group, dtype=left_inv.dtype))]
  transfers between devices with their start and end apart: 11 -> 10, of which waited for: 6 -> 6; matrix products, arithmetic and copies ran while one was open for 8% -> 2% of each run, Pallas kernels for 19% -> 19%
where the time goes in v4:
time: 137 us; the launch traced here: 136 us
  waiting for transfers between devices  66.7 us (49%)
  Pallas kernels  37.5 us (27%)
  starting transfers between devices  26.5 us (19%)
  local copies, waits for them, and re-layouts  3.56 us (3%)
    ppermute x8, waiting for transfers between devices, swap(): return lax.ppermute(values, 'docs', [(i, i ^ k) for i in range(devices)])  55.5 us
    ppermute x8, starting transfers between devices, swap(): return lax.ppermute(values, 'docs', [(i, i ^ k) for i in range(devices)])  14.8 us
    pallas_call x1, Pallas kernels, precondition(): call(kernel, jax.ShapeDtypeStruct(queries.shape, queries.dtype), (total /...  13 us
    all_to_all x1, waiting for transfers between devices, on_device(): lax.all_to_all(picked, 'docs', split_axis=0, concat_axis=0, axis_index_gr...  7.73 us
    all_to_all x1, starting transfers between devices, on_device(): lax.all_to_all(jnp.broadcast_to(own_ids, (devices, 1, entries)), 'docs',...  7.39 us
    pallas_call x1, Pallas kernels, gather_rows(): call(kernel, pltpu.HBM((count, features, entries), tables[0].dtype), (cou...  6.56 us
    pallas_call x1, Pallas kernels, score_near(): call(kernel, jax.ShapeDtypeStruct((queries, entries), jnp.float32), (coun...  6.37 us
    pallas_call x2, Pallas kernels, gather_pieces(): call(kernel, [pltpu.HBM((features, entries), table.dtype)] * count, (1,),...  6.29 us
  transfers between devices with their start and end apart: 10, of which 6 were waited for; matrix products, arithmetic and copies ran while one was open for 2% of the time, Pallas kernels for 19%

profile of v4, /device:TPU:0, one launch (start us, length us, event | category | flops | bytes accessed | tf_op | source)
XLA Modules:
  0.0 135.8 jit_solution(5108019788383061707)
XLA Ops:
  0.0 0.7 broadcast_multiply_fusion
  0.7 0.7 add.3
  1.4 0.6 broadcast_in_dim.3
  2.0 7.4 %all-to-all-start = ((s32[16,1,256]{2,1,0:T(1,128)}), s32[16,1,256]{2,1,0:T(1,128)S(1)}, u32[]{:S(2)}, u32[]{:S(2)}) async-start(s32[16,1,256]{2,1,0:T(1,128)} %broadcast_in_dim.3), calls=%async_computation | async-start | bytes 32768 | tf_op jit(solution)/shard_map/all_to_all | solution.py:281
  9.4 2.9 %copy.7 = bf16[2048,512]{0,1:T(8,128)(2,1)S(1)} copy(bf16[2048,512]{1,0:T(8,128)(2,1)} %param.6) | data formatting | bytes 4194304 | tf_op args[0]
  12.3 3.6 %all-to-all-done.refs_0_.refs_1_.ids_ref.refs_2_.refs_3_.refs_4_.refs_5_ = s32[16,1,256]{2,1,0:T(1,128)S(1)} async-done(((s32[16,1,256]{2,1,0:T(1,128)}), s32[16,1,256]{2,1,0:T(1,128)S(1)}, u32[]{:S(2)}, u32[]{:S(2)}) %all-to-all-start) | async-done | bytes 16416 | tf_op jit(solution)/shard_map/all_to_all | solution.py:281
  15.9 2.1 %shard_map.64 = (bf16[512,256]{1,0:T(8,128)(2,1)}, bf16[512,256]{1,0:T(8,128)(2,1)}) custom-call(s32[1]{0:T(128)} %bitcast.me_ref, s32[16,1,256]{2,1,0:T(1,128)S(1)} %all-to-all-done.refs_0_.refs_1_.ids_ref.refs_2_.refs_3_.refs_4_.refs_5_, s32[16,1,256]{2,1,0:T(1,128)S(1)} %all-to-all-done.refs_0_.refs_1_.ids_ref.refs_2_.refs_3_.refs_4_.refs_5_, ...), custom_call_target="tpu_custom_call" | custom-call | flops 1000 | bytes 1000 | tf_op jit(solution)/shard_map/pallas_call | solution.py:79
  17.9 0.5 collective-permute-start
  18.4 1.5 %collective-permute-start.1 = (bf16[512,256]{1,0:T(8,128)(2,1)}, bf16[512,256]{1,0:T(8,128)(2,1)S(1)}, u32[]{:S(2)}, u32[]{:S(2)}) collective-permute-start(bf16[512,256]{1,0:T(8,128)(2,1)} %get-tuple-element.18), channel_id=1, source_target_pairs={{0,9},{1,8},{2,11},{3,10},{4,13},{5,12},{6,15},{7,14},{8,1},{9,0},... | collective-permute-start | bytes 786440 | tf_op jit(solution)/shard_map/ppermute | solution.py:278
  19.9 18.7 %collective-permute-done.refs_4_ = bf16[512,256]{1,0:T(8,128)(2,1)S(1)} collective-permute-done((bf16[512,256]{1,0:T(8,128)(2,1)}, bf16[512,256]{1,0:T(8,128)(2,1)S(1)}, u32[]{:S(2)}, u32[]{:S(2)}) %collective-permute-start) | collective-permute-done | bytes 262176 | tf_op jit(solution)/shard_map/ppermute | solution.py:278
  38.6 4.9 %collective-permute-done.1.refs_5_ = bf16[512,256]{1,0:T(8,128)(2,1)S(1)} collective-permute-done((bf16[512,256]{1,0:T(8,128)(2,1)}, bf16[512,256]{1,0:T(8,128)(2,1)S(1)}, u32[]{:S(2)}, u32[]{:S(2)}) %collective-permute-start.1) | collective-permute-done | bytes 262176 | tf_op jit(solution)/shard_map/ppermute | solution.py:278
  43.5 6.6 %shard_map.65 = bf16[8,512,256]{2,1,0:T(8,128)(2,1)} custom-call(s32[1]{0:T(128)S(6)} %and.4.base_ref, s32[16,1,256]{2,1,0:T(1,128)S(1)} %all-to-all-done.refs_0_.refs_1_.ids_ref.refs_2_.refs_3_.refs_4_.refs_5_, bf16[512,2048]{1,0:T(8,128)(2,1)S(1)} %bitcast.4), custom_call_target="tpu_custom_call" | custom-call | flops 1000 | bytes 1000 | tf_op jit(solution)/shard_map/pallas_call | solution.py:56
  50.0 4.3 %all-to-all-start.1 = ((bf16[8,512,256]{2,1,0:T(8,128)(2,1)}), bf16[8,512,256]{2,1,0:T(8,128)(2,1)}, u32[]{:S(2)}, u32[]{:S(2)}) async-start(bf16[8,512,256]{2,1,0:T(8,128)(2,1)} %shard_map.65), calls=%async_computation.1 | async-start | bytes 4194304 | tf_op jit(solution)/shard_map/all_to_all | solution.py:302
  54.4 0.0 copy-start
  54.4 0.0 copy-start.1
  54.4 4.2 %shard_map.66 = (bf16[512,256]{1,0:T(8,128)(2,1)}, bf16[512,256]{1,0:T(8,128)(2,1)}, bf16[512,256]{1,0:T(8,128)(2,1)}, bf16[512,256]{1,0:T(8,128)(2,1)}, bf16[51...) custom-call(s32[1]{0:T(128)} %bitcast.me_ref, ...), custom_call_target="tpu_custom_call" | custom-call | flops 1000 | bytes 1000 | tf_op jit(solution)/shard_map/pallas_call | solution.py:79
  58.7 1.3 collective-permute-start.2
  60.0 3.8 %collective-permute-start.3 = (bf16[512,256]{1,0:T(8,128)(2,1)}, bf16[512,256]{1,0:T(8,128)(2,1)S(1)}, u32[]{:S(2)}, u32[]{:S(2)}) collective-permute-start(bf16[512,256]{1,0:T(8,128)(2,1)} %get-tuple-element.22), channel_id=1, source_target_pairs={{0,12},{1,13},{2,14},{3,15},{4,8},{5,9},{6,10},{7,11},{8,4},{9,5},... | collective-permute-start | bytes 786440 | tf_op jit(solution)/shard_map/ppermute | solution.py:278
  63.8 0.0 collective-permute-start.4
  63.8 3.0 %collective-permute-start.5 = (bf16[512,256]{1,0:T(8,128)(2,1)}, bf16[512,256]{1,0:T(8,128)(2,1)S(1)}, u32[]{:S(2)}, u32[]{:S(2)}) collective-permute-start(bf16[512,256]{1,0:T(8,128)(2,1)} %get-tuple-element.24), channel_id=1, source_target_pairs={{0,14},{1,15},{2,12},{3,13},{4,10},{5,11},{6,8},{7,9},{8,6},{9,7},... | collective-permute-start | bytes 786440 | tf_op jit(solution)/shard_map/ppermute | solution.py:278
  66.8 1.2 collective-permute-start.6
  68.0 15.9 %collective-permute-done.2.refs_6_ = bf16[512,256]{1,0:T(8,128)(2,1)S(1)} collective-permute-done((bf16[512,256]{1,0:T(8,128)(2,1)}, bf16[512,256]{1,0:T(8,128)(2,1)S(1)}, u32[]{:S(2)}, u32[]{:S(2)}) %collective-permute-start.2) | collective-permute-done | bytes 262176 | tf_op jit(solution)/shard_map/ppermute | solution.py:278
  83.9 3.4 %collective-permute-start.7 = (bf16[512,256]{1,0:T(8,128)(2,1)}, bf16[512,256]{1,0:T(8,128)(2,1)S(1)}, u32[]{:S(2)}, u32[]{:S(2)}) collective-permute-start(bf16[512,256]{1,0:T(8,128)(2,1)} %get-tuple-element.26), channel_id=1, source_target_pairs={{0,11},{1,10},{2,9},{3,8},{4,15},{5,14},{6,13},{7,12},{8,3},{9,2},... | collective-permute-start | bytes 786440 | tf_op jit(solution)/shard_map/ppermute | solution.py:278
  87.3 0.0 copy-done
  87.3 0.0 copy-done.1
  87.3 13.0 %shard_map.67.prepared_ref.refs_0_.refs_1_.refs_2_.refs_3_ = bf16[512,8192]{1,0:T(8,128)(2,1)} custom-call(bf16[512,8192]{1,0:T(8,128)(2,1)} %queries_ref, bf16[2,32,32]{2,1,0:T(8,128)(2,1)S(1)} %copy-done.1, bf16[2,128,128]{2,1,0:T(8,128)(2,1)S(1)} %copy-done), custom_call_target="tpu_custom_call" | custom-call | flops 4294967296 | bytes 16777216 | tf_op jit(solution)/shard_map/pallas_call | solution.py:243
  100.4 7.7 %all-to-all-done.1.chosen_ref = bf16[8,512,256]{2,1,0:T(8,128)(2,1)} async-done(((bf16[8,512,256]{2,1,0:T(8,128)(2,1)}), bf16[8,512,256]{2,1,0:T(8,128)(2,1)}, u32[]{:S(2)}, u32[]{:S(2)}) %all-to-all-start.1) | async-done | bytes 2097184 | tf_op jit(solution)/shard_map/all_to_all | solution.py:302
  108.1 6.4 %shard_map.68.refs_8_ = f32[512,256]{1,0:T(8,128)S(1)} custom-call(s32[1]{0:T(128)S(6)} %and.4.base_ref, bf16[512,8192]{1,0:T(8,128)(2,1)} %shard_map.67.prepared_ref.refs_0_.refs_1_.refs_2_.refs_3_, bf16[8,512,256]{2,1,0:T(8,128)(2,1)} %all-to-all-done.1.chosen_ref), custom_call_target="tpu_custom_call" | custom-call | flops 1073741824 | bytes 6815744 | tf_op jit(solution)/shard_map/pallas_call | solution.py:107
  114.5 16.0 %collective-permute-done.7.refs_7_ = bf16[512,256]{1,0:T(8,128)(2,1)S(1)} collective-permute-done((bf16[512,256]{1,0:T(8,128)(2,1)}, bf16[512,256]{1,0:T(8,128)(2,1)S(1)}, u32[]{:S(2)}, u32[]{:S(2)}) %collective-permute-start.7) | collective-permute-done | bytes 262176 | tf_op jit(solution)/shard_map/ppermute | solution.py:278
  130.5 2.2 %shard_map.69.refs_8_ = f32[512,256]{1,0:T(8,128)S(1)} custom-call(s32[1]{0:T(128)} %bitcast.me_ref, bf16[512,8192]{1,0:T(8,128)(2,1)} %shard_map.67.prepared_ref.refs_0_.refs_1_.refs_2_.refs_3_, bf16[512,8192]{1,0:T(8,128)(2,1)} %shard_map.67.prepared_ref.refs_0_.refs_1_.refs_2_.refs_3_, ...), custom_call_target="tpu_custom_call" | custom-call | flops 536870912 | bytes 4194304 | tf_op jit(solution)/shard_map/pallas_call | solution.py:134
  132.7 0.0 collective-permute-done.3.refs_4_
  132.7 0.0 collective-permute-done.4.refs_5_
  132.8 0.0 collective-permute-done.5.refs_6_
  132.8 0.0 collective-permute-done.6.refs_7_
  132.8 3.0 %shard_map.70 = f32[512,256]{1,0:T(8,128)} custom-call(s32[1]{0:T(128)} %bitcast.me_ref, bf16[512,8192]{1,0:T(8,128)(2,1)} %shard_map.67.prepared_ref.refs_0_.refs_1_.refs_2_.refs_3_, bf16[512,8192]{1,0:T(8,128)(2,1)} %shard_map.67.prepared_ref.refs_0_.refs_1_.refs_2_.refs_3_, bf16[512,8192]{1,0:T(8,128)(2,1)} %shard_map.67.prepared_ref.refs_0_.refs_1_.refs_2_.refs_3_, ...), custom_call_target="tpu_custom_call" | custom-call | flops 536870912 | bytes 4194304 | tf_op jit(solution)/shard_map/pallas_call | solution.py:134
Async XLA Ops:
  2.0 13.9 %all-to-all-start = ((s32[16,1,256]{2,1,0:T(1,128)}), s32[16,1,256]{2,1,0:T(1,128)S(1)}, u32[]{:S(2)}, u32[]{:S(2)}) async-start(s32[16,1,256]{2,1,0:T(1,128)} %broadcast_in_dim.3), calls=%async_computation | async-start | bytes 32768 | tf_op jit(solution)/shard_map/all_to_all | solution.py:281
  17.9 20.7 %collective-permute-start = (bf16[512,256]{1,0:T(8,128)(2,1)}, bf16[512,256]{1,0:T(8,128)(2,1)S(1)}, u32[]{:S(2)}, u32[]{:S(2)}) collective-permute-start(bf16[512,256]{1,0:T(8,128)(2,1)} %get-tuple-element.16), channel_id=1, source_target_pairs={{0,8},{1,9},{2,10},{3,11},{4,12},{5,13},{6,14},{7,15},{8,0},{9,1},... | collective-permute-start | bytes 786440 | tf_op jit(solution)/shard_map/ppermute | solution.py:278
  18.4 25.1 %collective-permute-start.1 = (bf16[512,256]{1,0:T(8,128)(2,1)}, bf16[512,256]{1,0:T(8,128)(2,1)S(1)}, u32[]{:S(2)}, u32[]{:S(2)}) collective-permute-start(bf16[512,256]{1,0:T(8,128)(2,1)} %get-tuple-element.18), channel_id=1, source_target_pairs={{0,9},{1,8},{2,11},{3,10},{4,13},{5,12},{6,15},{7,14},{8,1},{9,0},... | collective-permute-start | bytes 786440 | tf_op jit(solution)/shard_map/ppermute | solution.py:278
  50.0 58.0 %all-to-all-start.1 = ((bf16[8,512,256]{2,1,0:T(8,128)(2,1)}), bf16[8,512,256]{2,1,0:T(8,128)(2,1)}, u32[]{:S(2)}, u32[]{:S(2)}) async-start(bf16[8,512,256]{2,1,0:T(8,128)(2,1)} %shard_map.65), calls=%async_computation.1 | async-start | bytes 4194304 | tf_op jit(solution)/shard_map/all_to_all | solution.py:302
  54.4 32.9 %copy-start = (bf16[2,128,128]{2,1,0:T(8,128)(2,1)S(1)}, bf16[2,128,128]{2,1,0:T(8,128)(2,1)}, u32[]{:S(2)}) copy-start(bf16[2,128,128]{2,1,0:T(8,128)(2,1)} %right_inv_ref.1) | copy-start | bytes 196612
  54.4 32.9 %copy-start.1 = (bf16[2,32,32]{2,1,0:T(8,128)(2,1)S(1)}, bf16[2,32,32]{2,1,0:T(8,128)(2,1)}, u32[]{:S(2)}) copy-start(bf16[2,32,32]{2,1,0:T(8,128)(2,1)} %left_inv_ref.1) | copy-start | bytes 12292
  58.7 25.2 %collective-permute-start.2 = (bf16[512,256]{1,0:T(8,128)(2,1)}, bf16[512,256]{1,0:T(8,128)(2,1)S(1)}, u32[]{:S(2)}, u32[]{:S(2)}) collective-permute-start(bf16[512,256]{1,0:T(8,128)(2,1)} %get-tuple-element.20), channel_id=1, source_target_pairs={{0,10},{1,11},{2,8},{3,9},{4,14},{5,15},{6,12},{7,13},{8,2},{9,3},... | collective-permute-start | bytes 786440 | tf_op jit(solution)/shard_map/ppermute | solution.py:278
  60.0 72.7 %collective-permute-start.3 = (bf16[512,256]{1,0:T(8,128)(2,1)}, bf16[512,256]{1,0:T(8,128)(2,1)S(1)}, u32[]{:S(2)}, u32[]{:S(2)}) collective-permute-start(bf16[512,256]{1,0:T(8,128)(2,1)} %get-tuple-element.22), channel_id=1, source_target_pairs={{0,12},{1,13},{2,14},{3,15},{4,8},{5,9},{6,10},{7,11},{8,4},{9,5},... | collective-permute-start | bytes 786440 | tf_op jit(solution)/shard_map/ppermute | solution.py:278
  63.8 68.9 %collective-permute-start.4 = (bf16[512,256]{1,0:T(8,128)(2,1)}, bf16[512,256]{1,0:T(8,128)(2,1)S(1)}, u32[]{:S(2)}, u32[]{:S(2)}) collective-permute-start(bf16[512,256]{1,0:T(8,128)(2,1)} %get-tuple-element.23), channel_id=1, source_target_pairs={{0,13},{1,12},{2,15},{3,14},{4,9},{5,8},{6,11},{7,10},{8,5},{9,4},... | collective-permute-start | bytes 786440 | tf_op jit(solution)/shard_map/ppermute | solution.py:278
  63.8 68.9 %collective-permute-start.5 = (bf16[512,256]{1,0:T(8,128)(2,1)}, bf16[512,256]{1,0:T(8,128)(2,1)S(1)}, u32[]{:S(2)}, u32[]{:S(2)}) collective-permute-start(bf16[512,256]{1,0:T(8,128)(2,1)} %get-tuple-element.24), channel_id=1, source_target_pairs={{0,14},{1,15},{2,12},{3,13},{4,10},{5,11},{6,8},{7,9},{8,6},{9,7},... | collective-permute-start | bytes 786440 | tf_op jit(solution)/shard_map/ppermute | solution.py:278
  66.8 65.9 %collective-permute-start.6 = (bf16[512,256]{1,0:T(8,128)(2,1)}, bf16[512,256]{1,0:T(8,128)(2,1)S(1)}, u32[]{:S(2)}, u32[]{:S(2)}) collective-permute-start(bf16[512,256]{1,0:T(8,128)(2,1)} %get-tuple-element.25), channel_id=1, source_target_pairs={{0,15},{1,14},{2,13},{3,12},{4,11},{5,10},{6,9},{7,8},{8,7},{9,6},... | collective-permute-start | bytes 786440 | tf_op jit(solution)/shard_map/ppermute | solution.py:278
  83.9 46.6 %collective-permute-start.7 = (bf16[512,256]{1,0:T(8,128)(2,1)}, bf16[512,256]{1,0:T(8,128)(2,1)S(1)}, u32[]{:S(2)}, u32[]{:S(2)}) collective-permute-start(bf16[512,256]{1,0:T(8,128)(2,1)} %get-tuple-element.26), channel_id=1, source_target_pairs={{0,11},{1,10},{2,9},{3,8},{4,15},{5,14},{6,13},{7,12},{8,3},{9,2},... | collective-permute-start | bytes 786440 | tf_op jit(solution)/shard_map/ppermute | solution.py:278
